TPU v7x, 512 devices: a whole 4x4x16 slice. The times are simulated.
512 devices in a mesh: dp: 32 (over y, x, core), mp: 16 (over z).
Axes of the slice: x: 4, y: 4, z: 16, core: 2. Of those that a mesh axis runs over, the one named last changes fastest.
Arguments:
- tokens: bfloat16 [4096, 8192], P('dp', 'mp'), may hold values from -6 to 6
- cotangent: bfloat16 [4096, 8192], P('dp', 'mp'), may hold values from -6 to 6
- up_weight: bfloat16 [5, 256, 32768], P(None, 'dp', 'mp'), may hold values from -0.15625 to 0.15625
- down_weight: bfloat16 [5, 256, 32768], P(None, 'dp', 'mp'), may hold values from -0.078125 to 0.078125
Outputs:
- mixed: bfloat16 [4096, 8192], P('dp', 'mp')
- grad_tokens: bfloat16 [4096, 8192], P('dp', 'mp')
All inputs are finite; a program needn't handle non-finite values.
Results may differ from a plain program's by a relative error of at most 0.0049.
Values may be sent and summed in bfloat16 or wider, within the bound.
A program may use at most 64 MiB of HBM per device.

v0:
```python
import jax
import jax.numpy as jnp
from jax import lax
from jax.sharding import PartitionSpec as P

BLK = 256
LEVELS = 4


def partner(x, axis, stride):
    return lax.ppermute(x, axis, [(i, i ^ 1 << stride) for i in range(lax.axis_size(axis))])


def partner_blocks(blocks, block_bit, sender):
    block_count = blocks.shape[1]
    return sender(blocks, block_bit - (block_count.bit_length() - 1))


def per_bit(blocks, sender):
    return [partner_blocks(blocks, 1 + bit_pos, sender) for bit_pos in range(LEVELS)]


def by_levels(blocks, shuffled_list):
    return jnp.stack([blocks] + list(shuffled_list), axis=0)


def collect_terms(terms, sender):
    block_count = terms.shape[2]
    summed = terms[0]
    remote = []
    for bit_pos in range(LEVELS):
        block_bit = 1 + bit_pos
        remote.append((terms[1 + bit_pos], block_bit - (block_count.bit_length() - 1)))
    for blocks, device_bit in remote:
        summed = summed + sender(blocks, device_bit)
    return summed


def up_product(token_terms, up_all, block_count):
    term_count, blk_width, local_units = up_all.shape
    up_terms = up_all.reshape(term_count, blk_width, block_count, local_units // block_count)
    return jnp.einsum("stci,sicf->tcf", token_terms, up_terms, preferred_element_type=jnp.float32)


def on_device(tokens, cotangent, up_weight, down_weight):
    tok_rows = tokens.shape[0]
    block_count = tokens.shape[1] // BLK
    hidden_per = up_weight.shape[2] // block_count
    token_blocks = tokens.reshape(tok_rows, block_count, BLK)
    cot_blocks = cotangent.reshape(tok_rows, block_count, BLK)

    def token_sender(blocks, device_bit):
        return partner(blocks, "mp", device_bit)

    def cot_sender(blocks, device_bit):
        return partner(blocks, "mp", device_bit)

    token_list = per_bit(token_blocks, token_sender)
    cot_list = per_bit(cot_blocks, cot_sender)

    def term_sender(blocks, device_bit):
        return partner(blocks, "mp", device_bit)

    def grad_sender(blocks, device_bit):
        return partner(blocks, "mp", device_bit)

    token_terms = by_levels(token_blocks, token_list)
    up_all, down_all = (
        lax.all_gather(up_weight, "dp", axis=1, tiled=True),
        lax.all_gather(down_weight, "dp", axis=1, tiled=True),
    )
    pre_act = up_product(token_terms, up_all, block_count)
    term_count = up_all.shape[0]
    up_terms = up_all.reshape(term_count, BLK, block_count, hidden_per)
    down_terms = down_all.reshape(term_count, BLK, block_count, hidden_per)
    hidden = jax.nn.gelu(pre_act).astype(jnp.bfloat16)
    out_terms = jnp.einsum("tcf,sjcf->stcj", hidden, down_terms, preferred_element_type=jnp.float32)
    mixed = collect_terms(out_terms, term_sender)
    cot_terms = by_levels(cot_blocks, cot_list)
    grad_hidden = jnp.einsum(
        "stcj,sjcf->tcf", cot_terms, down_terms, preferred_element_type=jnp.float32
    )
    grad_pre = jax.vjp(jax.nn.gelu, pre_act)[1](grad_hidden)[0].astype(jnp.bfloat16)
    grad_terms = jnp.einsum(
        "tcf,sicf->stci", grad_pre, up_terms, preferred_element_type=jnp.float32
    )
    grad_tokens = collect_terms(grad_terms, grad_sender)
    return (
        mixed.reshape(tok_rows, -1).astype(jnp.bfloat16),
        grad_tokens.reshape(tok_rows, -1).astype(jnp.bfloat16),
    )


def solution(mesh):
    in_specs = (P("dp", "mp"), P("dp", "mp"), P(None, "dp", "mp"), P(None, "dp", "mp"))
    out_specs = (P("dp", "mp"), P("dp", "mp"))
    return jax.shard_map(
        on_device, mesh=mesh, in_specs=in_specs, out_specs=out_specs, check_vma=False
    )
```

profile of v0, /device:TPU:32, one launch (start us, length us, event | category | flops | bytes accessed | tf_op | source)
XLA Modules:
  0.0 276.3 jit_solution(12114262262853458736)
XLA Ops:
  7.2 0.0 all-gather.3.cloned.1.call-start
  7.2 0.7 all-gather.3.cloned.1.call-update
  7.9 0.0 all-gather.5.cloned.1.call-start
  7.9 0.7 all-gather.5.cloned.1.call-update
  8.6 1.0 copy.68
  9.7 0.1 copy.70
  9.8 14.8 %collective-permute-start.11 = (bf16[128,2,256]{2,0,1:T(8,128)(2,1)S(1)}, bf16[128,2,256]{2,0,1:T(8,128)(2,1)S(1)}, u32[]{:S(2)}, u32[]{:S(2)}) collective-permute-start(bf16[128,2,256]{2,0,1:T(8,128)(2,1)S(1)} %copy.70), channel_id=1, source_target_pairs={{0,8},{1,9},{2,10},{3,11},{4,12},{5,13},{6,14},{7,15},{8,0},{9,1},... | collective-permute-start | bytes 393224 | tf_op jit(solution)/shard_map/ppermute | solution.py:11
  24.6 4.3 %collective-permute-start.10 = (bf16[128,2,256]{2,0,1:T(8,128)(2,1)S(1)}, bf16[128,2,256]{2,0,1:T(8,128)(2,1)S(1)}, u32[]{:S(2)}, u32[]{:S(2)}) collective-permute-start(bf16[128,2,256]{2,0,1:T(8,128)(2,1)S(1)} %copy.70), channel_id=1, source_target_pairs={{0,4},{1,5},{2,6},{3,7},{4,0},{5,1},{6,2},{7,3},{8,12},{9,13},{10,... | collective-permute-start | bytes 393224 | tf_op jit(solution)/shard_map/ppermute | solution.py:11
  28.9 3.4 %collective-permute-start.9 = (bf16[128,2,256]{2,0,1:T(8,128)(2,1)S(1)}, bf16[128,2,256]{2,0,1:T(8,128)(2,1)S(1)}, u32[]{:S(2)}, u32[]{:S(2)}) collective-permute-start(bf16[128,2,256]{2,0,1:T(8,128)(2,1)S(1)} %copy.70), channel_id=1, source_target_pairs={{0,2},{1,3},{2,0},{3,1},{4,6},{5,7},{6,4},{7,5},{8,10},{9,11},{10,... | collective-permute-start | bytes 393224 | tf_op jit(solution)/shard_map/ppermute | solution.py:11
  32.3 2.9 %collective-permute-start.8 = (bf16[128,2,256]{2,0,1:T(8,128)(2,1)S(1)}, bf16[128,2,256]{2,0,1:T(8,128)(2,1)S(1)}, u32[]{:S(2)}, u32[]{:S(2)}) collective-permute-start(bf16[128,2,256]{2,0,1:T(8,128)(2,1)S(1)} %copy.70), channel_id=1, source_target_pairs={{0,1},{1,0},{2,3},{3,2},{4,5},{5,4},{6,7},{7,6},{8,9},{9,8},{10,11... | collective-permute-start | bytes 393224 | tf_op jit(solution)/shard_map/ppermute | solution.py:11
  35.2 1.0 copy.52
  36.3 0.1 copy.54
  36.4 2.9 %collective-permute-start = (bf16[128,2,256]{2,0,1:T(8,128)(2,1)S(1)}, bf16[128,2,256]{2,0,1:T(8,128)(2,1)S(1)}, u32[]{:S(2)}, u32[]{:S(2)}) collective-permute-start(bf16[128,2,256]{2,0,1:T(8,128)(2,1)S(1)} %copy.54), channel_id=1, source_target_pairs={{0,1},{1,0},{2,3},{3,2},{4,5},{5,4},{6,7},{7,6},{8,9},{9,8},{10,11... | collective-permute-start | bytes 393224 | tf_op jit(solution)/shard_map/ppermute | solution.py:11
  39.3 0.1 copy.58
  39.5 0.1 copy.74
  39.6 0.7 constant_dynamic-update-slice_fusion.1
  40.3 6.6 %collective-permute-done = bf16[128,2,256]{2,0,1:T(8,128)(2,1)S(1)} collective-permute-done((bf16[128,2,256]{2,0,1:T(8,128)(2,1)S(1)}, bf16[128,2,256]{2,0,1:T(8,128)(2,1)S(1)}, u32[]{:S(2)}, u32[]{:S(2)}) %collective-permute-start) | collective-permute-done | bytes 131104 | tf_op jit(solution)/shard_map/ppermute | solution.py:11
  46.8 10.0 %collective-permute-start.1 = (bf16[128,2,256]{2,0,1:T(8,128)(2,1)S(1)}, bf16[128,2,256]{2,0,1:T(8,128)(2,1)S(1)}, u32[]{:S(2)}, u32[]{:S(2)}) collective-permute-start(bf16[128,2,256]{2,0,1:T(8,128)(2,1)S(1)} %copy.54), channel_id=1, source_target_pairs={{0,2},{1,3},{2,0},{3,1},{4,6},{5,7},{6,4},{7,5},{8,10},{9,11},{10,... | collective-permute-start | bytes 393224 | tf_op jit(solution)/shard_map/ppermute | solution.py:11
  56.8 5.5 %collective-permute-done.1 = bf16[128,2,256]{2,0,1:T(8,128)(2,1)S(1)} collective-permute-done((bf16[128,2,256]{2,0,1:T(8,128)(2,1)S(1)}, bf16[128,2,256]{2,0,1:T(8,128)(2,1)S(1)}, u32[]{:S(2)}, u32[]{:S(2)}) %collective-permute-start.1) | collective-permute-done | bytes 131104 | tf_op jit(solution)/shard_map/ppermute | solution.py:11
  62.3 3.9 %collective-permute-start.2 = (bf16[128,2,256]{2,0,1:T(8,128)(2,1)S(1)}, bf16[128,2,256]{2,0,1:T(8,128)(2,1)S(1)}, u32[]{:S(2)}, u32[]{:S(2)}) collective-permute-start(bf16[128,2,256]{2,0,1:T(8,128)(2,1)S(1)} %copy.54), channel_id=1, source_target_pairs={{0,4},{1,5},{2,6},{3,7},{4,0},{5,1},{6,2},{7,3},{8,12},{9,13},{10,... | collective-permute-start | bytes 393224 | tf_op jit(solution)/shard_map/ppermute | solution.py:11
  66.2 11.9 %collective-permute-done.2 = bf16[128,2,256]{2,0,1:T(8,128)(2,1)S(1)} collective-permute-done((bf16[128,2,256]{2,0,1:T(8,128)(2,1)S(1)}, bf16[128,2,256]{2,0,1:T(8,128)(2,1)S(1)}, u32[]{:S(2)}, u32[]{:S(2)}) %collective-permute-start.2) | collective-permute-done | bytes 131104 | tf_op jit(solution)/shard_map/ppermute | solution.py:11
  78.2 3.2 %collective-permute-start.3 = (bf16[128,2,256]{2,0,1:T(8,128)(2,1)S(1)}, bf16[128,2,256]{2,0,1:T(8,128)(2,1)S(1)}, u32[]{:S(2)}, u32[]{:S(2)}) collective-permute-start(bf16[128,2,256]{2,0,1:T(8,128)(2,1)S(1)} %copy.54), channel_id=1, source_target_pairs={{0,8},{1,9},{2,10},{3,11},{4,12},{5,13},{6,14},{7,15},{8,0},{9,1},... | collective-permute-start | bytes 393224 | tf_op jit(solution)/shard_map/ppermute | solution.py:11
  81.4 18.7 %collective-permute-done.3 = bf16[128,2,256]{2,0,1:T(8,128)(2,1)S(1)} collective-permute-done((bf16[128,2,256]{2,0,1:T(8,128)(2,1)S(1)}, bf16[128,2,256]{2,0,1:T(8,128)(2,1)S(1)}, u32[]{:S(2)}, u32[]{:S(2)}) %collective-permute-start.3) | collective-permute-done | bytes 131104 | tf_op jit(solution)/shard_map/ppermute | solution.py:11
  100.1 0.0 collective-permute-done.8
  100.1 0.7 bitcast_dynamic-update-slice_fusion.3
  100.8 0.0 collective-permute-done.9
  100.8 0.7 bitcast_dynamic-update-slice_fusion.2
  101.5 0.0 collective-permute-done.10
  101.5 0.7 bitcast_dynamic-update-slice_fusion.1
  102.2 0.0 collective-permute-done.11
  102.2 0.7 bitcast_dynamic-update-slice_fusion
  102.8 0.0 all-gather.3.cloned.1.call-done
  102.8 7.9 %copy.59 = bf16[5,256,2048]{1,2,0:T(8,128)(2,1)} copy(bf16[5,256,2048]{2,1,0:T(8,128)(2,1)} %all-gather.3.cloned.1.call-done) | data formatting | bytes 10485760 | tf_op jit(solution)/shard_map/all_gather | solution.py:69
  110.7 4.3 %fusion.14 = f32[128,2,1024]{2,0,1:T(8,128)S(1)} fusion(bf16[5,128,2,256]{3,1,0,2:T(8,128)(2,1)S(1)} %bitcast_dynamic-update-slice_fusion.4, bf16[5,256,2,1024]{1,3,2,0:T(8,128)(2,1)} %bitcast.113), kind=kOutput, calls=%fused_computation.12 | convolution fusion | flops 671088640 | bytes 6946816 | tf_op jit(solution)/shard_map/stci,sicf->tcf/dot_general | solution.py:42
  115.0 0.0 copy-start
  115.0 28.5 %all-gather.5.cloned.1.call-done = bf16[5,256,2048]{2,1,0:T(8,128)(2,1)} async-done(((bf16[5,8,2048]{2,1,0:T(8,128)(2,1)}), bf16[5,256,2048]{2,1,0:T(8,128)(2,1)}) %all-gather.5.cloned.1.call-update) | async-done | bytes 5242896 | tf_op jit(solution)/shard_map/all_gather | solution.py:70
  143.5 7.9 %copy.61 = bf16[5,256,2048]{1,2,0:T(8,128)(2,1)} copy(bf16[5,256,2048]{2,1,0:T(8,128)(2,1)} %all-gather.5.cloned.1.call-done) | data formatting | bytes 10485760 | tf_op jit(solution)/shard_map/all_gather | solution.py:70
  151.4 0.0 copy-done
  151.4 3.5 %fusion.11 = f32[5,128,2,256]{3,1,0,2:T(8,128)S(1)} fusion(bf16[5,256,2,1024]{1,3,2,0:T(8,128)(2,1)} %bitcast.115, f32[128,2,1024]{2,0,1:T(8,128)S(1)} %fusion.14), kind=kOutput, calls=%fused_computation.11 | convolution fusion | flops 673447936 | bytes 7602176 | tf_op jit(solution)/shard_map/tcf,sjcf->stcj/dot_general | solution.py:77
  154.9 1.0 slice_bitcast_fusion.8
  155.9 2.4 collective-permute-start.4
  158.3 4.4 %collective-permute-start.5 = (f32[128,2,256]{2,0,1:T(8,128)}, f32[128,2,256]{2,0,1:T(8,128)S(1)}, u32[]{:S(2)}, u32[]{:S(2)}) collective-permute-start(f32[128,2,256]{2,0,1:T(8,128)} %get-tuple-element.11), channel_id=1, source_target_pairs={{0,2},{1,3},{2,0},{3,1},{4,6},{5,7},{6,4},{7,5},{8,10},{9,11},{10,... | collective-permute-start | bytes 786440 | tf_op jit(solution)/shard_map/ppermute | solution.py:11
  162.7 11.0 %collective-permute-start.7 = (f32[128,2,256]{2,0,1:T(8,128)}, f32[128,2,256]{2,0,1:T(8,128)}, u32[]{:S(2)}, u32[]{:S(2)}) collective-permute-start(f32[128,2,256]{2,0,1:T(8,128)} %get-tuple-element.12), channel_id=1, source_target_pairs={{0,8},{1,9},{2,10},{3,11},{4,12},{5,13},{6,14},{7,15},{8,0},{9,1},... | collective-permute-start | bytes 786440 | tf_op jit(solution)/shard_map/ppermute | solution.py:11
  173.8 2.8 %collective-permute-start.6 = (f32[128,2,256]{2,0,1:T(8,128)}, f32[128,2,256]{2,0,1:T(8,128)}, u32[]{:S(2)}, u32[]{:S(2)}) collective-permute-start(f32[128,2,256]{2,0,1:T(8,128)} %get-tuple-element.13), channel_id=1, source_target_pairs={{0,4},{1,5},{2,6},{3,7},{4,0},{5,1},{6,2},{7,3},{8,12},{9,13},{10,... | collective-permute-start | bytes 786440 | tf_op jit(solution)/shard_map/ppermute | solution.py:11
  176.6 7.2 %fusion.8 = f32[5,128,2,256]{3,1,0,2:T(8,128)S(1)} fusion(bf16[5,256,2,1024]{1,3,2,0:T(8,128)(2,1)} %bitcast.114, f32[128,2,1024]{2,0,1:T(8,128)} %copy-done, bf16[5,128,2,256]{3,1,0,2:T(8,128)(2,1)} %bitcast_dynamic-update-slice_fusion, bf16[5,256,2,1024]{1,3,2,0:T(8,128)(2,1)} %bitcast.116), kind=kOutput, calls=%fused_computation.10 | convolution fusion | flops 1347420160 | bytes 13500416 | tf_op jit(solution)/shard_map/tcf,sicf->stci/dot_general | solution.py:84
  183.8 1.0 slice_bitcast_fusion.3
  184.9 2.6 collective-permute-start.12
  187.4 0.0 collective-permute-done.4
  187.4 4.1 %collective-permute-start.13 = (f32[128,2,256]{2,0,1:T(8,128)}, f32[128,2,256]{2,0,1:T(8,128)}, u32[]{:S(2)}, u32[]{:S(2)}) collective-permute-start(f32[128,2,256]{2,0,1:T(8,128)} %get-tuple-element.7), channel_id=1, source_target_pairs={{0,2},{1,3},{2,0},{3,1},{4,6},{5,7},{6,4},{7,5},{8,10},{9,11},{10,... | collective-permute-start | bytes 786440 | tf_op jit(solution)/shard_map/ppermute | solution.py:11
  191.5 10.9 %collective-permute-done.5 = f32[128,2,256]{2,0,1:T(8,128)S(1)} collective-permute-done((f32[128,2,256]{2,0,1:T(8,128)}, f32[128,2,256]{2,0,1:T(8,128)S(1)}, u32[]{:S(2)}, u32[]{:S(2)}) %collective-permute-start.5) | collective-permute-done | bytes 262176 | tf_op jit(solution)/shard_map/ppermute | solution.py:11
  202.4 12.1 %collective-permute-start.15 = (f32[128,2,256]{2,0,1:T(8,128)}, f32[128,2,256]{2,0,1:T(8,128)}, u32[]{:S(2)}, u32[]{:S(2)}) collective-permute-start(f32[128,2,256]{2,0,1:T(8,128)} %get-tuple-element.8), channel_id=1, source_target_pairs={{0,8},{1,9},{2,10},{3,11},{4,12},{5,13},{6,14},{7,15},{8,0},{9,1},... | collective-permute-start | bytes 786440 | tf_op jit(solution)/shard_map/ppermute | solution.py:11
  214.5 0.0 collective-permute-done.7
  214.5 1.9 collective-permute-start.14
  216.4 14.4 %collective-permute-done.6 = f32[128,2,256]{2,0,1:T(8,128)} collective-permute-done((f32[128,2,256]{2,0,1:T(8,128)}, f32[128,2,256]{2,0,1:T(8,128)}, u32[]{:S(2)}, u32[]{:S(2)}) %collective-permute-start.6) | collective-permute-done | bytes 262176 | tf_op jit(solution)/shard_map/ppermute | solution.py:11
  230.8 1.1 fusion.49
  231.9 0.1 copy.67
  232.0 0.8 copy.82
  232.8 0.0 collective-permute-done.12
  232.8 5.9 %collective-permute-done.13 = f32[128,2,256]{2,0,1:T(8,128)} collective-permute-done((f32[128,2,256]{2,0,1:T(8,128)}, f32[128,2,256]{2,0,1:T(8,128)}, u32[]{:S(2)}, u32[]{:S(2)}) %collective-permute-start.13) | collective-permute-done | bytes 262176 | tf_op jit(solution)/shard_map/ppermute | solution.py:11
  238.7 0.0 collective-permute-done.15
  238.7 28.7 %collective-permute-done.14 = f32[128,2,256]{2,0,1:T(8,128)} collective-permute-done((f32[128,2,256]{2,0,1:T(8,128)}, f32[128,2,256]{2,0,1:T(8,128)}, u32[]{:S(2)}, u32[]{:S(2)}) %collective-permute-start.14) | collective-permute-done | bytes 262176 | tf_op jit(solution)/shard_map/ppermute | solution.py:11
  267.3 1.2 fusion.44
  268.5 0.1 copy.81
  268.6 0.8 copy.83
  (5 shorter events, 0.1 us)
Async XLA Ops:
  7.2 95.7 %all-gather.3.cloned.1.call-start = ((), (), s32[]{:S(2)}) async-start(), calls=%async_computation | async-start | bytes 5406720 | tf_op jit(solution)/shard_map/all_gather | solution.py:69
  7.9 135.7 %all-gather.5.cloned.1.call-start = ((), (), s32[]{:S(2)}) async-start(), calls=%async_computation.1 | async-start | bytes 5406720 | tf_op jit(solution)/shard_map/all_gather | solution.py:70
  9.8 92.4 %collective-permute-start.11 = (bf16[128,2,256]{2,0,1:T(8,128)(2,1)S(1)}, bf16[128,2,256]{2,0,1:T(8,128)(2,1)S(1)}, u32[]{:S(2)}, u32[]{:S(2)}) collective-permute-start(bf16[128,2,256]{2,0,1:T(8,128)(2,1)S(1)} %copy.70), channel_id=1, source_target_pairs={{0,8},{1,9},{2,10},{3,11},{4,12},{5,13},{6,14},{7,15},{8,0},{9,1},... | collective-permute-start | bytes 393224 | tf_op jit(solution)/shard_map/ppermute | solution.py:11
  24.6 76.9 %collective-permute-start.10 = (bf16[128,2,256]{2,0,1:T(8,128)(2,1)S(1)}, bf16[128,2,256]{2,0,1:T(8,128)(2,1)S(1)}, u32[]{:S(2)}, u32[]{:S(2)}) collective-permute-start(bf16[128,2,256]{2,0,1:T(8,128)(2,1)S(1)} %copy.70), channel_id=1, source_target_pairs={{0,4},{1,5},{2,6},{3,7},{4,0},{5,1},{6,2},{7,3},{8,12},{9,13},{10,... | collective-permute-start | bytes 393224 | tf_op jit(solution)/shard_map/ppermute | solution.py:11
  28.9 71.9 %collective-permute-start.9 = (bf16[128,2,256]{2,0,1:T(8,128)(2,1)S(1)}, bf16[128,2,256]{2,0,1:T(8,128)(2,1)S(1)}, u32[]{:S(2)}, u32[]{:S(2)}) collective-permute-start(bf16[128,2,256]{2,0,1:T(8,128)(2,1)S(1)} %copy.70), channel_id=1, source_target_pairs={{0,2},{1,3},{2,0},{3,1},{4,6},{5,7},{6,4},{7,5},{8,10},{9,11},{10,... | collective-permute-start | bytes 393224 | tf_op jit(solution)/shard_map/ppermute | solution.py:11
  32.3 67.8 %collective-permute-start.8 = (bf16[128,2,256]{2,0,1:T(8,128)(2,1)S(1)}, bf16[128,2,256]{2,0,1:T(8,128)(2,1)S(1)}, u32[]{:S(2)}, u32[]{:S(2)}) collective-permute-start(bf16[128,2,256]{2,0,1:T(8,128)(2,1)S(1)} %copy.70), channel_id=1, source_target_pairs={{0,1},{1,0},{2,3},{3,2},{4,5},{5,4},{6,7},{7,6},{8,9},{9,8},{10,11... | collective-permute-start | bytes 393224 | tf_op jit(solution)/shard_map/ppermute | solution.py:11
  36.4 10.4 %collective-permute-start = (bf16[128,2,256]{2,0,1:T(8,128)(2,1)S(1)}, bf16[128,2,256]{2,0,1:T(8,128)(2,1)S(1)}, u32[]{:S(2)}, u32[]{:S(2)}) collective-permute-start(bf16[128,2,256]{2,0,1:T(8,128)(2,1)S(1)} %copy.54), channel_id=1, source_target_pairs={{0,1},{1,0},{2,3},{3,2},{4,5},{5,4},{6,7},{7,6},{8,9},{9,8},{10,11... | collective-permute-start | bytes 393224 | tf_op jit(solution)/shard_map/ppermute | solution.py:11
  46.8 15.5 %collective-permute-start.1 = (bf16[128,2,256]{2,0,1:T(8,128)(2,1)S(1)}, bf16[128,2,256]{2,0,1:T(8,128)(2,1)S(1)}, u32[]{:S(2)}, u32[]{:S(2)}) collective-permute-start(bf16[128,2,256]{2,0,1:T(8,128)(2,1)S(1)} %copy.54), channel_id=1, source_target_pairs={{0,2},{1,3},{2,0},{3,1},{4,6},{5,7},{6,4},{7,5},{8,10},{9,11},{10,... | collective-permute-start | bytes 393224 | tf_op jit(solution)/shard_map/ppermute | solution.py:11
  62.3 15.8 %collective-permute-start.2 = (bf16[128,2,256]{2,0,1:T(8,128)(2,1)S(1)}, bf16[128,2,256]{2,0,1:T(8,128)(2,1)S(1)}, u32[]{:S(2)}, u32[]{:S(2)}) collective-permute-start(bf16[128,2,256]{2,0,1:T(8,128)(2,1)S(1)} %copy.54), channel_id=1, source_target_pairs={{0,4},{1,5},{2,6},{3,7},{4,0},{5,1},{6,2},{7,3},{8,12},{9,13},{10,... | collective-permute-start | bytes 393224 | tf_op jit(solution)/shard_map/ppermute | solution.py:11
  78.2 22.0 %collective-permute-start.3 = (bf16[128,2,256]{2,0,1:T(8,128)(2,1)S(1)}, bf16[128,2,256]{2,0,1:T(8,128)(2,1)S(1)}, u32[]{:S(2)}, u32[]{:S(2)}) collective-permute-start(bf16[128,2,256]{2,0,1:T(8,128)(2,1)S(1)} %copy.54), channel_id=1, source_target_pairs={{0,8},{1,9},{2,10},{3,11},{4,12},{5,13},{6,14},{7,15},{8,0},{9,1},... | collective-permute-start | bytes 393224 | tf_op jit(solution)/shard_map/ppermute | solution.py:11
  115.0 36.4 %copy-start = (f32[128,2,1024]{2,0,1:T(8,128)}, f32[128,2,1024]{2,0,1:T(8,128)S(1)}, u32[]{:S(2)}) copy-start(f32[128,2,1024]{2,0,1:T(8,128)S(1)} %fusion.14) | copy-start | bytes 3145732
  155.9 31.5 %collective-permute-start.4 = (f32[128,2,256]{2,0,1:T(8,128)}, f32[128,2,256]{2,0,1:T(8,128)S(1)}, u32[]{:S(2)}, u32[]{:S(2)}) collective-permute-start(f32[128,2,256]{2,0,1:T(8,128)} %get-tuple-element.10), channel_id=1, source_target_pairs={{0,1},{1,0},{2,3},{3,2},{4,5},{5,4},{6,7},{7,6},{8,9},{9,8},{10,11... | collective-permute-start | bytes 786440 | tf_op jit(solution)/shard_map/ppermute | solution.py:11
  158.3 44.1 %collective-permute-start.5 = (f32[128,2,256]{2,0,1:T(8,128)}, f32[128,2,256]{2,0,1:T(8,128)S(1)}, u32[]{:S(2)}, u32[]{:S(2)}) collective-permute-start(f32[128,2,256]{2,0,1:T(8,128)} %get-tuple-element.11), channel_id=1, source_target_pairs={{0,2},{1,3},{2,0},{3,1},{4,6},{5,7},{6,4},{7,5},{8,10},{9,11},{10,... | collective-permute-start | bytes 786440 | tf_op jit(solution)/shard_map/ppermute | solution.py:11
  162.7 51.7 %collective-permute-start.7 = (f32[128,2,256]{2,0,1:T(8,128)}, f32[128,2,256]{2,0,1:T(8,128)}, u32[]{:S(2)}, u32[]{:S(2)}) collective-permute-start(f32[128,2,256]{2,0,1:T(8,128)} %get-tuple-element.12), channel_id=1, source_target_pairs={{0,8},{1,9},{2,10},{3,11},{4,12},{5,13},{6,14},{7,15},{8,0},{9,1},... | collective-permute-start | bytes 786440 | tf_op jit(solution)/shard_map/ppermute | solution.py:11
  173.8 57.0 %collective-permute-start.6 = (f32[128,2,256]{2,0,1:T(8,128)}, f32[128,2,256]{2,0,1:T(8,128)}, u32[]{:S(2)}, u32[]{:S(2)}) collective-permute-start(f32[128,2,256]{2,0,1:T(8,128)} %get-tuple-element.13), channel_id=1, source_target_pairs={{0,4},{1,5},{2,6},{3,7},{4,0},{5,1},{6,2},{7,3},{8,12},{9,13},{10,... | collective-permute-start | bytes 786440 | tf_op jit(solution)/shard_map/ppermute | solution.py:11
  184.9 47.9 %collective-permute-start.12 = (f32[128,2,256]{2,0,1:T(8,128)}, f32[128,2,256]{2,0,1:T(8,128)S(1)}, u32[]{:S(2)}, u32[]{:S(2)}) collective-permute-start(f32[128,2,256]{2,0,1:T(8,128)} %get-tuple-element.6), channel_id=1, source_target_pairs={{0,1},{1,0},{2,3},{3,2},{4,5},{5,4},{6,7},{7,6},{8,9},{9,8},{10,11... | collective-permute-start | bytes 786440 | tf_op jit(solution)/shard_map/ppermute | solution.py:11
  187.4 51.2 %collective-permute-start.13 = (f32[128,2,256]{2,0,1:T(8,128)}, f32[128,2,256]{2,0,1:T(8,128)}, u32[]{:S(2)}, u32[]{:S(2)}) collective-permute-start(f32[128,2,256]{2,0,1:T(8,128)} %get-tuple-element.7), channel_id=1, source_target_pairs={{0,2},{1,3},{2,0},{3,1},{4,6},{5,7},{6,4},{7,5},{8,10},{9,11},{10,... | collective-permute-start | bytes 786440 | tf_op jit(solution)/shard_map/ppermute | solution.py:11
  202.4 36.3 %collective-permute-start.15 = (f32[128,2,256]{2,0,1:T(8,128)}, f32[128,2,256]{2,0,1:T(8,128)}, u32[]{:S(2)}, u32[]{:S(2)}) collective-permute-start(f32[128,2,256]{2,0,1:T(8,128)} %get-tuple-element.8), channel_id=1, source_target_pairs={{0,8},{1,9},{2,10},{3,11},{4,12},{5,13},{6,14},{7,15},{8,0},{9,1},... | collective-permute-start | bytes 786440 | tf_op jit(solution)/shard_map/ppermute | solution.py:11
  214.5 52.9 %collective-permute-start.14 = (f32[128,2,256]{2,0,1:T(8,128)}, f32[128,2,256]{2,0,1:T(8,128)}, u32[]{:S(2)}, u32[]{:S(2)}) collective-permute-start(f32[128,2,256]{2,0,1:T(8,128)} %get-tuple-element.9), channel_id=1, source_target_pairs={{0,4},{1,5},{2,6},{3,7},{4,0},{5,1},{6,2},{7,3},{8,12},{9,13},{10,... | collective-permute-start | bytes 786440 | tf_op jit(solution)/shard_map/ppermute | solution.py:11
Sparse Core Ops, SparseCore 0:
  11.2 66.8 all-gather.2
  81.3 62.2 all-gather.4
where the time goes:
time: 277 us; the launch traced here: 276 us
  waiting for transfers between devices  132 us (48%)
  starting transfers between devices  86.8 us (31%)
  local copies, waits for them, and re-layouts  25.5 us (9%)
  matrix products  15 us (5%)
  between operations  14.3 us (5%)
    ppermute x16, waiting for transfers between devices, partner(): lax.ppermute(x, axis, [(i, i ^ 1 << stride) for i in range(lax.axis_size(...  103 us
    ppermute x16, starting transfers between devices, partner(): lax.ppermute(x, axis, [(i, i ^ 1 << stride) for i in range(lax.axis_size(...  86.7 us
    all_gather x1, waiting for transfers between devices, on_device(): lax.all_gather(down_weight, 'dp', axis=1, tiled=True)  28.5 us
    all_gather x1, local copies, waits for them, and re-layouts, on_device(): lax.all_gather(up_weight, 'dp', axis=1, tiled=True)  7.89 us
    all_gather x1, local copies, waits for them, and re-layouts, on_device(): lax.all_gather(down_weight, 'dp', axis=1, tiled=True)  7.87 us
    dot_general x1, matrix products, on_device(): jnp.einsum('tcf,sicf->stci', grad_pre, up_terms, preferred_element_type=j...  7.23 us
    unnamed x14, local copies, waits for them, and re-layouts  6.34 us
  transfers between devices with their start and end apart: 18, of which 9 were waited for; matrix products, arithmetic and copies ran while one was open for 10% of the time, Pallas kernels for 0%

commit v1 on v0

v1 whole, which is shorter than its diff:
```python
import math

import jax
import jax.numpy as jnp
from jax import lax
from jax.experimental import pallas as pl
from jax.experimental.pallas import tpu as pltpu
from jax.sharding import PartitionSpec as P

BLK = 256
TERMS = 5
HB = 1024
TOK = 128
SIDE = 4
MESH = pl.DeviceIdType.MESH
ROOT = math.sqrt(2.0 / math.pi)
CUBE = 0.044715

Q4, Q2, Q1A, Q1B, Q0A, Q0B, Q0C = range(7)


def xor_step(bit, amount):
    return amount - 2 * amount * bit


class Sends:
    def __init__(self, send_sem, recv_sem):
        self.send_sem, self.recv_sem = send_sem, recv_sem
        self.sent, self.received, self.open = 0, 0, []

    def slot(self):
        self.received += 1
        return self.received - 1

    def copy(self, src, dst, slot, device):
        copy = pltpu.make_async_remote_copy(
            src_ref=src, dst_ref=dst, send_sem=self.send_sem.at[self.sent],
            recv_sem=self.recv_sem.at[slot], device_id=device, device_id_type=MESH,
        )
        self.sent += 1
        return copy

    def start(self, src, dst, slot, device, when=None):
        copy = self.copy(src, dst, slot, device)
        self.open.append((copy, when))
        if when is None:
            copy.start()
        else:
            pl.when(when)(copy.start)

    def arrive(self, dst, slot, device):
        pltpu.make_async_remote_copy(
            src_ref=dst, dst_ref=dst, send_sem=self.send_sem.at[0],
            recv_sem=self.recv_sem.at[slot], device_id=device, device_id_type=MESH,
        ).wait_recv()

    def drain(self):
        for copy, when in self.open:
            if when is None:
                copy.wait_send()
            else:
                pl.when(when)(copy.wait_send)
        self.open = []


def kernel(tok, cot, up, down, out_mixed, out_grad,
           x_all, c_all, wu, wd, stage, terms, sendbuf, landed, hidden, slope, gpre,
           local_sem, send_sem, recv_sem):
    dp = lax.axis_index("dp")
    z = lax.axis_index("mp")
    core = lax.rem(dp, 2)
    chip = lax.div(dp, 2)
    px, py = lax.rem(chip, SIDE), lax.div(chip, SIDE)
    a = px * (1 - core) + py * core
    b = py * (1 - core) + px * core

    def chip_at(a_pos, b_pos):
        return a_pos * (1 + 3 * core) + b_pos * (4 - 3 * core)

    def ring(pos, step):
        return lax.rem(pos + step + SIDE, SIDE)

    def plane(a_pos, b_pos):
        return (chip_at(a_pos, b_pos) * 2 + core, z)

    b0 = lax.rem(z, 2)
    b1 = lax.rem(lax.div(z, 2), 2)
    b2 = lax.rem(lax.div(z, 4), 2)
    b3 = lax.rem(lax.div(z, 8), 2)
    d1, d2, d4, d8 = xor_step(b0, 1), xor_step(b1, 2), xor_step(b2, 4), xor_step(b3, 8)
    c01 = b0 != b1
    c12 = b1 != b2
    c02 = b0 != b2
    n01 = b0 == b1
    far = jnp.logical_and(c12, c02)
    mid4 = jnp.logical_and(b1 == b2, c02)
    own4 = jnp.logical_and(b1 == b2, b0 == b2)

    def along(step):
        return (dp, z + step)

    sibling = (dp + 1 - 2 * core, z)
    sends = Sends(send_sem, recv_sem)

    mine = pl.ds(pl.multiple_of(core * BLK, BLK), BLK)
    theirs = pl.ds(pl.multiple_of((1 - core) * BLK, BLK), BLK)
    own_rows = pl.ds(pl.multiple_of(core * TOK, TOK), TOK)
    sib_rows = pl.ds(pl.multiple_of((1 - core) * TOK, TOK), TOK)
    own_units = pl.ds(pl.multiple_of(core * HB, HB), HB)
    sib_units = pl.ds(pl.multiple_of((1 - core) * HB, HB), HB)
    acts, alls = (tok, cot), (x_all, c_all)
    weights, gathered = (up, down), (wu, wd)

    local = []
    for n in range(2):
        local.append(pltpu.make_async_copy(acts[n].at[:, mine], alls[n].at[0, own_rows, :], local_sem.at[n]))
        local.append(pltpu.make_async_copy(weights[n].at[:, :, own_units], stage.at[n, 0], local_sem.at[2 + n]))
    for copy in local:
        copy.start()

    barrier = pltpu.get_barrier_semaphore()
    a_up, a_down, b_up, b_down = (
        plane(ring(a, 1), b), plane(ring(a, -1), b), plane(a, ring(b, 1)), plane(a, ring(b, -1)))
    greet = [sibling, a_up, a_down, b_up, b_down]
    greet += [along(s) for s in (d1, d2, d4, d1 + d2, d1 + d4, d2 + d4, d4 + d8)]
    for device in greet:
        pl.semaphore_signal(barrier, inc=1, device_id=device, device_id_type=MESH)
    pl.semaphore_wait(barrier, len(greet))

    swap_act = [sends.slot() for _ in range(2)]
    swap_w = [sends.slot() for _ in range(2)]
    for n in range(2):
        sends.start(acts[n].at[:, theirs], alls[n].at[0, own_rows, :], swap_act[n], sibling)
        sends.start(weights[n].at[:, :, sib_units], stage.at[n, 1], swap_w[n], sibling)

    act_slot = [[[sends.slot() for _ in range(5)] for _ in range(2)] for _ in range(2)]
    act_rows = (own_rows, sib_rows)

    def act_send(n, ch, src, dst, device, when=None):
        rows = act_rows[ch]
        sends.start(alls[n].at[src, rows, :], alls[n].at[dst, rows, :], act_slot[n][ch][dst], device, when)

    def act_wait(n, ch, dst):
        sends.arrive(alls[n].at[dst, act_rows[ch], :], act_slot[n][ch][dst], sibling)

    def act_own(n, ch):
        if ch == 0:
            local[2 * n].wait()
        else:
            sends.arrive(alls[n].at[0, sib_rows, :], swap_act[n], sibling)
        act_send(n, ch, 0, 1, along(d1))
        act_send(n, ch, 0, 2, along(d2), c01)
        act_send(n, ch, 0, 3, along(d4), far)

    def act_one(n, ch):
        act_wait(n, ch, 1)
        act_send(n, ch, 1, 2, along(d1 + d2), c01)
        act_send(n, ch, 1, 3, along(d1 + d4), far)

    def act_two(n, ch):
        act_wait(n, ch, 2)
        act_send(n, ch, 2, 3, along(d2 + d4), c12)

    def act_four(n, ch):
        act_wait(n, ch, 3)
        act_send(n, ch, 3, 4, along(d4 + d8))

    def act_end(n, ch):
        act_wait(n, ch, 4)

    w_slot = [[sends.slot() for _ in range(20)] for _ in range(2)]
    ks = (a, ring(a, -1), ring(a, 1), ring(a, 2))
    lo, hi, whole = pl.ds(0, HB // 2), pl.ds(HB // 2, HB // 2), pl.ds(0, HB)

    def piece(n, a_pos, b_pos, cols):
        rows = pl.ds(pl.multiple_of(chip_at(a_pos, b_pos) * 16, 16), 16)
        return gathered[n].at[:, rows, cols]

    def w_send(n, a_pos, b_pos, cols, slot, device):
        ref = piece(n, a_pos, b_pos, cols)
        sends.start(ref, ref, w_slot[n][slot], device)

    def w_wait(n, a_pos, b_pos, cols, slot):
        sends.arrive(piece(n, a_pos, b_pos, cols), w_slot[n][slot], sibling)

    def w_across(n, k):
        w_send(n, ks[k], b, whole, 4 + k, b_up)
        w_send(n, ks[k], b, whole, 8 + k, b_down)

    def w_start(n):
        local[2 * n + 1].wait()
        sends.arrive(stage.at[n, 1], swap_w[n], sibling)
        first = stage[n, 0].astype(jnp.float32)
        second = stage[n, 1].astype(jnp.float32)
        rows = pl.ds(pl.multiple_of(chip * 16, 16), 16)

        @pl.when(core == 0)
        def _():
            gathered[n][:, rows, :] = jnp.concatenate([first, second], axis=1).astype(jnp.bfloat16)

        @pl.when(core == 1)
        def _():
            gathered[n][:, rows, :] = jnp.concatenate([second, first], axis=1).astype(jnp.bfloat16)

        w_send(n, a, b, whole, 0, a_up)
        w_send(n, a, b, whole, 1, a_down)
        w_across(n, 0)

    def w_near(n):
        w_wait(n, ks[1], b, whole, 0)
        w_send(n, ks[1], b, lo, 2, a_up)
        w_wait(n, ks[2], b, whole, 1)
        w_send(n, ks[2], b, hi, 3, a_down)
        w_across(n, 1)
        w_across(n, 2)

    def w_far(n):
        w_wait(n, ks[3], b, lo, 2)
        w_wait(n, ks[3], b, hi, 3)
        w_across(n, 3)

    def w_pass(n, k):
        w_wait(n, ks[k], ring(b, -1), whole, 4 + k)
        w_send(n, ks[k], ring(b, -1), lo, 12 + k, b_up)
        w_wait(n, ks[k], ring(b, 1), whole, 8 + k)
        w_send(n, ks[k], ring(b, 1), hi, 16 + k, b_down)

    def w_end(n):
        for k in range(4):
            w_wait(n, ks[k], ring(b, 2), lo, 12 + k)
            w_wait(n, ks[k], ring(b, 2), hi, 16 + k)

    TILE = 256

    def product(all_ref, w_ref, cols):
        total = None
        for s in range(TERMS):
            part = jnp.dot(all_ref[s], w_ref[s, :, cols], preferred_element_type=jnp.float32)
            total = part if total is None else total + part
        return total

    def forward():
        def body(tile, carry):
            cols = pl.ds(pl.multiple_of(tile * TILE, TILE), TILE)
            pre = product(x_all, wu, cols)
            th = jnp.tanh(ROOT * (pre + CUBE * pre * pre * pre))
            hidden[:, cols] = (0.5 * pre * (1.0 + th)).astype(jnp.bfloat16)
            inner = ROOT * (1.0 + 3.0 * CUBE * pre * pre)
            slope[:, cols] = 0.5 * (1.0 + th) + 0.5 * pre * (1.0 - th * th) * inner
            return carry
        lax.fori_loop(0, HB // TILE, body, 0)

    def backward():
        def body(tile, carry):
            cols = pl.ds(pl.multiple_of(tile * TILE, TILE), TILE)
            gpre[:, cols] = (product(c_all, wd, cols) * slope[:, cols]).astype(jnp.bfloat16)
            return carry
        lax.fori_loop(0, HB // TILE, body, 0)

    def term(o, s):
        act_ref, w_ref = ((hidden, wd), (gpre, wu))[o]
        terms[o, s] = lax.dot_general(
            act_ref[...], w_ref[s], (((1,), (1,)), ((), ())), preferred_element_type=jnp.float32)

    sum_slot = [[[sends.slot() for _ in range(7)] for _ in range(2)] for _ in range(2)]
    out_slot = [sends.slot() for _ in range(2)]
    sum_rows = (sib_rows, own_rows)
    outs = (out_mixed, out_grad)
    last = []

    def sum_send(o, ch, s, place, device, when=None):
        rows = sum_rows[ch]
        sends.start(sendbuf.at[o, s, rows, :], landed.at[o, place, rows, :], sum_slot[o][ch][place], device, when)

    def sum_add(o, ch, s, place, when=None):
        rows = sum_rows[ch]

        def add():
            sends.arrive(landed.at[o, place, rows, :], sum_slot[o][ch][place], sibling)
            terms[o, s, rows, :] += landed[o, place, rows, :].astype(jnp.float32)
        if when is None:
            add()
        else:
            pl.when(when)(add)

    def sum_round(o, ch, s):
        rows = sum_rows[ch]
        sendbuf[o, s, rows, :] = terms[o, s, rows, :].astype(jnp.bfloat16)

    def sum_eight(o, ch):
        sum_round(o, ch, 4)
        sum_send(o, ch, 4, Q4, along(d4 + d8))

    def sum_four(o, ch):
        sum_add(o, ch, 3, Q4)
        sum_round(o, ch, 3)
        sum_send(o, ch, 3, Q2, along(d2 + d4), c12)
        sum_send(o, ch, 3, Q1B, along(d1 + d4), mid4)
        sum_send(o, ch, 3, Q0C, along(d4), own4)

    def sum_two(o, ch):
        sum_add(o, ch, 2, Q2, c12)
        sum_round(o, ch, 2)
        sum_send(o, ch, 2, Q1A, along(d1 + d2), c01)
        sum_send(o, ch, 2, Q0B, along(d2), n01)

    def sum_one(o, ch):
        sum_add(o, ch, 1, Q1A, c01)
        sum_add(o, ch, 1, Q1B, far)
        sum_round(o, ch, 1)
        sum_send(o, ch, 1, Q0A, along(d1))

    def sum_own(o, ch):
        sum_add(o, ch, 0, Q0A)
        sum_add(o, ch, 0, Q0B, c01)
        sum_add(o, ch, 0, Q0C, far)
        sum_round(o, ch, 0)
        if ch == 0:
            sends.start(sendbuf.at[o, 0, sib_rows, :], outs[o].at[:, mine], out_slot[o], sibling)
        else:
            copy = pltpu.make_async_copy(sendbuf.at[o, 0, own_rows, :], outs[o].at[:, mine], local_sem.at[4 + o])
            copy.start()
            last.append(copy)

    T, C = 0, 1
    act_own(T, 0)
    w_start(0)
    act_own(T, 1)
    act_one(T, 0)
    w_near(0)
    act_own(C, 0)
    act_one(T, 1)
    act_two(T, 0)
    w_far(0)
    w_pass(0, 0)
    w_start(1)
    act_own(C, 1)
    act_one(C, 0)
    act_two(T, 1)
    act_four(T, 0)
    w_pass(0, 1)
    w_near(1)
    act_one(C, 1)
    act_two(C, 0)
    act_four(T, 1)
    w_pass(0, 2)
    w_pass(0, 3)
    w_far(1)
    act_two(C, 1)
    act_four(C, 0)
    w_end(0)
    w_pass(1, 0)
    w_pass(1, 1)
    act_end(T, 0)
    act_end(T, 1)
    act_four(C, 1)
    forward()
    w_pass(1, 2)
    w_pass(1, 3)
    w_end(1)
    for s in (4, 3):
        term(0, s)
        if s == 4:
            sum_eight(0, 0)
            sum_eight(0, 1)
    act_end(C, 0)
    act_end(C, 1)
    backward()
    term(1, 4)
    sum_eight(1, 0)
    sum_eight(1, 1)
    term(0, 2)
    sum_four(0, 0)
    term(0, 1)
    sum_four(0, 1)
    term(0, 0)
    sum_two(0, 0)
    term(1, 3)
    sum_two(0, 1)
    sum_four(1, 0)
    term(1, 2)
    sum_one(0, 0)
    sum_four(1, 1)
    term(1, 1)
    sum_one(0, 1)
    sum_two(1, 0)
    term(1, 0)
    sum_own(0, 0)
    sum_two(1, 1)
    sum_one(1, 0)
    sum_own(0, 1)
    sum_one(1, 1)
    sum_own(1, 0)
    sum_own(1, 1)
    for o in range(2):
        sends.arrive(outs[o].at[:, theirs], out_slot[o], sibling)
    for copy in last:
        copy.wait()
    sends.drain()
    assert sends.sent <= 160 and sends.received <= 160


def on_device(tokens, cotangent, up_weight, down_weight):
    any_spec = pl.BlockSpec(memory_space=pl.ANY)
    bf, f32 = jnp.bfloat16, jnp.float32
    return pl.pallas_call(
        kernel,
        out_shape=[jax.ShapeDtypeStruct(tokens.shape, bf)] * 2,
        in_specs=[any_spec] * 4,
        out_specs=[any_spec] * 2,
        scratch_shapes=[
            pltpu.VMEM((TERMS, 2 * TOK, BLK), bf),
            pltpu.VMEM((TERMS, 2 * TOK, BLK), bf),
            pltpu.VMEM((TERMS, BLK, HB), bf),
            pltpu.VMEM((TERMS, BLK, HB), bf),
            pltpu.VMEM((2, 2, TERMS, 8, HB), bf),
            pltpu.VMEM((2, TERMS, 2 * TOK, BLK), f32),
            pltpu.VMEM((2, TERMS, 2 * TOK, BLK), bf),
            pltpu.VMEM((2, 7, 2 * TOK, BLK), bf),
            pltpu.VMEM((2 * TOK, HB), bf),
            pltpu.VMEM((2 * TOK, HB), f32),
            pltpu.VMEM((2 * TOK, HB), bf),
            pltpu.SemaphoreType.DMA((6,)),
            pltpu.SemaphoreType.DMA((160,)),
            pltpu.SemaphoreType.DMA((160,)),
        ],
        compiler_params=pltpu.CompilerParams(
            collective_id=0, has_side_effects=True, vmem_limit_bytes=48 * 1024 * 1024),
    )(tokens, cotangent, up_weight, down_weight)


def solution(mesh):
    act, weight = P("dp", "mp"), P(None, "dp", "mp")
    return jax.shard_map(
        on_device, mesh=mesh, in_specs=(act, act, weight, weight), out_specs=(act, act), check_vma=False)
```

time: 277 us -> 110 us (0.40)
  the two profiles are of different devices: /device:TPU:32 before, /device:TPU:65 now
where the time goes in v1:
time: 110 us; the launch traced here: 109 us
  Pallas kernels  104 us (95%)
  local copies, waits for them, and re-layouts  4.94 us (4%)
    pallas_call x1, Pallas kernels, on_device(): pl.pallas_call(kernel, out_shape=[jax.ShapeDtypeStruct(tokens.shape, bf)]...  104 us
    unnamed x10, local copies, waits for them, and re-layouts  4.94 us

profile of v1, /device:TPU:65, one launch (start us, length us, event | category | flops | bytes accessed | tf_op | source)
XLA Modules:
  0.0 109.5 jit_solution(10151188161953433293)
XLA Ops:
  0.6 0.0 copy-start
  0.6 0.9 copy-done
  1.5 0.0 copy-start.1
  1.5 0.9 copy-done.1
  2.5 0.0 copy-start.2
  2.5 0.9 copy-done.2
  3.4 0.0 copy-start.3
  3.4 0.9 copy-done.3
  4.3 103.9 %shard_map.59 = (bf16[128,512]{1,0:T(8,128)(2,1)S(1)}, bf16[128,512]{1,0:T(8,128)(2,1)S(1)}) custom-call(bf16[128,512]{1,0:T(8,128)(2,1)S(1)} %copy-done.2, bf16[128,512]{1,0:T(8,128)(2,1)S(1)} %copy-done.3, bf16[5,8,2048]{2,1,0:T(8,128)(2,1)S(1)} %copy-done, bf16[5,8,2048]{2,1,0:T(8,128)(2,1)S(1)} %copy-done.1), custom_call_target="tpu_custom_call" | custom-call | tf_op jit(solution)/shard_map/pallas_call | solution.py:406
  108.2 0.7 copy.8
  108.8 0.7 copy.9
Async XLA Ops:
  0.6 0.9 copy-start
  1.5 0.9 copy-start.1
  2.5 0.9 copy-start.2
  3.4 0.9 copy-start.3

commit v2 on v1

--- a/solution.py
+++ b/solution.py
@@ -16,7 +16,7 @@
 ROOT = math.sqrt(2.0 / math.pi)
 CUBE = 0.044715
 
-Q4, Q2, Q1A, Q1B, Q0A, Q0B, Q0C = range(7)
+Q4, Q0A, Q0B, Q0C = range(4)
 
 
 def xor_step(bit, amount):
@@ -88,13 +88,6 @@
     b2 = lax.rem(lax.div(z, 4), 2)
     b3 = lax.rem(lax.div(z, 8), 2)
     d1, d2, d4, d8 = xor_step(b0, 1), xor_step(b1, 2), xor_step(b2, 4), xor_step(b3, 8)
-    c01 = b0 != b1
-    c12 = b1 != b2
-    c02 = b0 != b2
-    n01 = b0 == b1
-    far = jnp.logical_and(c12, c02)
-    mid4 = jnp.logical_and(b1 == b2, c02)
-    own4 = jnp.logical_and(b1 == b2, b0 == b2)
 
     def along(step):
         return (dp, z + step)
@@ -122,7 +115,7 @@
     a_up, a_down, b_up, b_down = (
         plane(ring(a, 1), b), plane(ring(a, -1), b), plane(a, ring(b, 1)), plane(a, ring(b, -1)))
     greet = [sibling, a_up, a_down, b_up, b_down]
-    greet += [along(s) for s in (d1, d2, d4, d1 + d2, d1 + d4, d2 + d4, d4 + d8)]
+    greet += [along(s) for s in (d1, d2, d4, d4 + d8)]
     for device in greet:
         pl.semaphore_signal(barrier, inc=1, device_id=device, device_id_type=MESH)
     pl.semaphore_wait(barrier, len(greet))
@@ -143,38 +136,19 @@
     def act_wait(n, ch, dst):
         sends.arrive(alls[n].at[dst, act_rows[ch], :], act_slot[n][ch][dst], sibling)
 
-    def act_own(n, ch):
-        if ch == 0:
-            local[2 * n].wait()
-        else:
-            sends.arrive(alls[n].at[0, sib_rows, :], swap_act[n], sibling)
-        act_send(n, ch, 0, 1, along(d1))
-        act_send(n, ch, 0, 2, along(d2), c01)
-        act_send(n, ch, 0, 3, along(d4), far)
-
-    def act_one(n, ch):
-        act_wait(n, ch, 1)
-        act_send(n, ch, 1, 2, along(d1 + d2), c01)
-        act_send(n, ch, 1, 3, along(d1 + d4), far)
-
-    def act_two(n, ch):
-        act_wait(n, ch, 2)
-        act_send(n, ch, 2, 3, along(d2 + d4), c12)
-
     def act_four(n, ch):
         act_wait(n, ch, 3)
         act_send(n, ch, 3, 4, along(d4 + d8))
 
-    def act_end(n, ch):
-        act_wait(n, ch, 4)
-
-    w_slot = [[sends.slot() for _ in range(20)] for _ in range(2)]
+    parts = ((0, 0, 5), (1, 3, 5), (1, 0, 3))
+    w_slot = [[sends.slot() for _ in range(20)] for _ in parts]
     ks = (a, ring(a, -1), ring(a, 1), ring(a, 2))
     lo, hi, whole = pl.ds(0, HB // 2), pl.ds(HB // 2, HB // 2), pl.ds(0, HB)
 
     def piece(n, a_pos, b_pos, cols):
         rows = pl.ds(pl.multiple_of(chip_at(a_pos, b_pos) * 16, 16), 16)
-        return gathered[n].at[:, rows, cols]
+        array, first, end = parts[n]
+        return gathered[array].at[first:end, rows, cols]
 
     def w_send(n, a_pos, b_pos, cols, slot, device):
         ref = piece(n, a_pos, b_pos, cols)
@@ -187,21 +161,22 @@
         w_send(n, ks[k], b, whole, 4 + k, b_up)
         w_send(n, ks[k], b, whole, 8 + k, b_down)
 
-    def w_start(n):
-        local[2 * n + 1].wait()
-        sends.arrive(stage.at[n, 1], swap_w[n], sibling)
-        first = stage[n, 0].astype(jnp.float32)
-        second = stage[n, 1].astype(jnp.float32)
+    def w_join(array):
+        local[2 * array + 1].wait()
+        sends.arrive(stage.at[array, 1], swap_w[array], sibling)
+        first = stage[array, 0].astype(jnp.float32)
+        second = stage[array, 1].astype(jnp.float32)
         rows = pl.ds(pl.multiple_of(chip * 16, 16), 16)
 
         @pl.when(core == 0)
         def _():
-            gathered[n][:, rows, :] = jnp.concatenate([first, second], axis=1).astype(jnp.bfloat16)
+            gathered[array][:, rows, :] = jnp.concatenate([first, second], axis=1).astype(jnp.bfloat16)
 
         @pl.when(core == 1)
         def _():
-            gathered[n][:, rows, :] = jnp.concatenate([second, first], axis=1).astype(jnp.bfloat16)
-
+            gathered[array][:, rows, :] = jnp.concatenate([second, first], axis=1).astype(jnp.bfloat16)
+
+    def w_start(n):
         w_send(n, a, b, whole, 0, a_up)
         w_send(n, a, b, whole, 1, a_down)
         w_across(n, 0)
@@ -262,7 +237,7 @@
         terms[o, s] = lax.dot_general(
             act_ref[...], w_ref[s], (((1,), (1,)), ((), ())), preferred_element_type=jnp.float32)
 
-    sum_slot = [[[sends.slot() for _ in range(7)] for _ in range(2)] for _ in range(2)]
+    sum_slot = [[[sends.slot() for _ in range(4)] for _ in range(2)] for _ in range(2)]
     out_slot = [sends.slot() for _ in range(2)]
     sum_rows = (sib_rows, own_rows)
     outs = (out_mixed, out_grad)
@@ -291,29 +266,7 @@
         sum_round(o, ch, 4)
         sum_send(o, ch, 4, Q4, along(d4 + d8))
 
-    def sum_four(o, ch):
-        sum_add(o, ch, 3, Q4)
-        sum_round(o, ch, 3)
-        sum_send(o, ch, 3, Q2, along(d2 + d4), c12)
-        sum_send(o, ch, 3, Q1B, along(d1 + d4), mid4)
-        sum_send(o, ch, 3, Q0C, along(d4), own4)
-
-    def sum_two(o, ch):
-        sum_add(o, ch, 2, Q2, c12)
-        sum_round(o, ch, 2)
-        sum_send(o, ch, 2, Q1A, along(d1 + d2), c01)
-        sum_send(o, ch, 2, Q0B, along(d2), n01)
-
-    def sum_one(o, ch):
-        sum_add(o, ch, 1, Q1A, c01)
-        sum_add(o, ch, 1, Q1B, far)
-        sum_round(o, ch, 1)
-        sum_send(o, ch, 1, Q0A, along(d1))
-
-    def sum_own(o, ch):
-        sum_add(o, ch, 0, Q0A)
-        sum_add(o, ch, 0, Q0B, c01)
-        sum_add(o, ch, 0, Q0C, far)
+    def out_send(o, ch):
         sum_round(o, ch, 0)
         if ch == 0:
             sends.start(sendbuf.at[o, 0, sib_rows, :], outs[o].at[:, mine], out_slot[o], sibling)
@@ -322,76 +275,112 @@
             copy.start()
             last.append(copy)
 
-    T, C = 0, 1
-    act_own(T, 0)
-    w_start(0)
-    act_own(T, 1)
-    act_one(T, 0)
-    w_near(0)
-    act_own(C, 0)
-    act_one(T, 1)
-    act_two(T, 0)
-    w_far(0)
-    w_pass(0, 0)
-    w_start(1)
-    act_own(C, 1)
-    act_one(C, 0)
-    act_two(T, 1)
-    act_four(T, 0)
-    w_pass(0, 1)
-    w_near(1)
-    act_one(C, 1)
-    act_two(C, 0)
-    act_four(T, 1)
-    w_pass(0, 2)
-    w_pass(0, 3)
-    w_far(1)
-    act_two(C, 1)
-    act_four(C, 0)
-    w_end(0)
-    w_pass(1, 0)
-    w_pass(1, 1)
-    act_end(T, 0)
-    act_end(T, 1)
-    act_four(C, 1)
+
+    def near_own(n, ch):
+        if ch == 0:
+            local[2 * n].wait()
+        else:
+            sends.arrive(alls[n].at[0, sib_rows, :], swap_act[n], sibling)
+        act_send(n, ch, 0, 3, along(d4))
+        act_send(n, ch, 0, 2, along(d2))
+        act_send(n, ch, 0, 1, along(d1))
+
+    def near_end(n, ch):
+        act_wait(n, ch, 1)
+        act_wait(n, ch, 2)
+        act_wait(n, ch, 4)
+
+    def near_two(o, ch):
+        sum_round(o, ch, 2)
+        sum_send(o, ch, 2, Q0B, along(d2))
+
+    def near_one(o, ch):
+        sum_round(o, ch, 1)
+        sum_send(o, ch, 1, Q0A, along(d1))
+
+    def near_four(o, ch):
+        sum_add(o, ch, 3, Q4)
+        sum_round(o, ch, 3)
+        sum_send(o, ch, 3, Q0C, along(d4))
+
+    def near_sum(o, ch):
+        sum_add(o, ch, 0, Q0A)
+        sum_add(o, ch, 0, Q0B)
+        sum_add(o, ch, 0, Q0C)
+        out_send(o, ch)
+
+    T, C, M, G = 0, 1, 0, 1
+    UP, DA, DB = 0, 1, 2
+    near_own(T,0)
+    w_join(0)
+    w_start(UP)
+    near_own(T,1)
+    w_near(UP)
+    w_pass(UP,0)
+    act_four(T,0)
+    w_far(UP)
+    act_four(T,1)
+    w_join(1)
+    w_start(DA)
+    near_own(C,0)
+    w_pass(UP,1)
+    w_pass(UP,2)
+    w_near(DA)
+    w_pass(DA,0)
+    near_own(C,1)
+    w_pass(UP,3)
+    w_far(DA)
+    w_pass(DA,1)
+    w_pass(DA,2)
+    w_start(DB)
+    w_end(UP)
+    w_pass(DA,3)
+    w_near(DB)
+    w_pass(DB,0)
+    act_four(C,0)
+    w_far(DB)
+    near_end(T,0)
+    near_end(T,1)
     forward()
-    w_pass(1, 2)
-    w_pass(1, 3)
-    w_end(1)
-    for s in (4, 3):
-        term(0, s)
-        if s == 4:
-            sum_eight(0, 0)
-            sum_eight(0, 1)
-    act_end(C, 0)
-    act_end(C, 1)
+    w_pass(DB,1)
+    w_pass(DB,2)
+    w_end(DA)
+    term(M,4)
+    sum_eight(M,0)
+    sum_eight(M,1)
+    term(M,3)
+    act_four(C,1)
+    w_pass(DB,3)
+    w_end(DB)
+    term(M,2)
+    near_two(M,0)
+    term(M,1)
+    near_one(M,0)
+    near_four(M,0)
+    near_two(M,1)
+    near_one(M,1)
+    near_four(M,1)
+    term(M,0)
+    near_end(C,0)
+    near_end(C,1)
     backward()
-    term(1, 4)
-    sum_eight(1, 0)
-    sum_eight(1, 1)
-    term(0, 2)
-    sum_four(0, 0)
-    term(0, 1)
-    sum_four(0, 1)
-    term(0, 0)
-    sum_two(0, 0)
-    term(1, 3)
-    sum_two(0, 1)
-    sum_four(1, 0)
-    term(1, 2)
-    sum_one(0, 0)
-    sum_four(1, 1)
-    term(1, 1)
-    sum_one(0, 1)
-    sum_two(1, 0)
-    term(1, 0)
-    sum_own(0, 0)
-    sum_two(1, 1)
-    sum_one(1, 0)
-    sum_own(0, 1)
-    sum_one(1, 1)
-    sum_own(1, 0)
-    sum_own(1, 1)
+    term(G,4)
+    sum_eight(G,0)
+    sum_eight(G,1)
+    term(G,2)
+    near_two(G,0)
+    term(G,3)
+    near_sum(M,0)
+    near_four(G,0)
+    near_two(G,1)
+    near_four(G,1)
+    term(G,1)
+    near_one(G,0)
+    near_one(G,1)
+    near_sum(M,1)
+    term(G,0)
+    near_sum(G,0)
+    near_sum(G,1)
     for o in range(2):
         sends.arrive(outs[o].at[:, theirs], out_slot[o], sibling)
     for copy in last:
@@ -416,7 +405,7 @@
             pltpu.VMEM((2, 2, TERMS, 8, HB), bf),
             pltpu.VMEM((2, TERMS, 2 * TOK, BLK), f32),
             pltpu.VMEM((2, TERMS, 2 * TOK, BLK), bf),
-            pltpu.VMEM((2, 7, 2 * TOK, BLK), bf),
+            pltpu.VMEM((2, 4, 2 * TOK, BLK), bf),
             pltpu.VMEM((2 * TOK, HB), bf),
             pltpu.VMEM((2 * TOK, HB), f32),
             pltpu.VMEM((2 * TOK, HB), bf),
@@ -425,7 +414,7 @@
             pltpu.SemaphoreType.DMA((160,)),
         ],
         compiler_params=pltpu.CompilerParams(
-            collective_id=0, has_side_effects=True, vmem_limit_bytes=48 * 1024 * 1024),
+            collective_id=0, has_side_effects=True, vmem_limit_bytes=60 * 1024 * 1024),
     )(tokens, cotangent, up_weight, down_weight)
 
 

time: 110 us -> 100 us (0.909)
  the two profiles are of different devices: /device:TPU:65 before, /device:TPU:32 now
where the time goes in v2:
time: 100 us; the launch traced here: 99.9 us
  Pallas kernels  97 us (97%)
  local copies, waits for them, and re-layouts  2.26 us (2%)
    pallas_call x1, Pallas kernels, on_device(): pl.pallas_call(kernel, out_shape=[jax.ShapeDtypeStruct(tokens.shape, bf)]...  97 us
    unnamed x4, local copies, waits for them, and re-layouts  2.26 us

profile of v2, /device:TPU:32, one launch (start us, length us, event | category | flops | bytes accessed | tf_op | source)
XLA Modules:
  0.0 99.9 jit_solution(13650544046485979951)
XLA Ops:
  0.6 97.0 %shard_map.59 = (bf16[128,512]{1,0:T(8,128)(2,1)}, bf16[128,512]{1,0:T(8,128)(2,1)}) custom-call(bf16[128,512]{1,0:T(8,128)(2,1)} %tok.1, bf16[128,512]{1,0:T(8,128)(2,1)} %cot.1, bf16[5,8,2048]{2,1,0:T(8,128)(2,1)} %up.1, bf16[5,8,2048]{2,1,0:T(8,128)(2,1)} %down.1), custom_call_target="tpu_custom_call" | custom-call | tf_op jit(solution)/shard_map/pallas_call | solution.py:395
  97.6 0.0 copy-start
  97.6 1.6 %copy.8 = bf16[128,512]{1,0:T(8,128)(2,1)} copy(bf16[128,512]{1,0:T(8,128)(2,1)} %get-tuple-element.4) | data formatting | bytes 262144
  99.2 0.0 copy-done
  99.2 0.7 copy.9
Async XLA Ops:
  97.6 1.6 %copy-start = (bf16[128,512]{1,0:T(8,128)(2,1)S(1)}, bf16[128,512]{1,0:T(8,128)(2,1)}, u32[]{:S(2)}) copy-start(bf16[128,512]{1,0:T(8,128)(2,1)} %get-tuple-element.5) | copy-start | bytes 393220

commit v3 on v2

v3 whole, which is shorter than its diff:
```python
import math

import jax
import jax.numpy as jnp
from jax import lax
from jax.experimental import pallas as pl
from jax.experimental.pallas import tpu as pltpu
from jax.sharding import PartitionSpec as P

BLK = 256
TERMS = 5
HB = 1024
TOK = 128
SIDE = 4
MESH = pl.DeviceIdType.MESH
ROOT = math.sqrt(2.0 / math.pi)
CUBE = 0.044715
SEND_SEMS, RECV_SEMS = 13, 58


def xor_step(bit, amount):
    return amount - 2 * amount * bit


class Sends:
    def __init__(self, send_sem, recv_sem):
        self.send_sem, self.recv_sem = send_sem, recv_sem
        self.groups, self.received = 0, 0

    def group(self):
        self.groups += 1
        return self.groups - 1

    def slot(self):
        self.received += 1
        return self.received - 1

    def start(self, src, dst, group, slot, device):
        pltpu.make_async_remote_copy(
            src_ref=src, dst_ref=dst, send_sem=self.send_sem.at[group],
            recv_sem=self.recv_sem.at[slot], device_id=device, device_id_type=MESH,
        ).start()

    def arrive(self, dst, slot, device):
        pltpu.make_async_remote_copy(
            src_ref=dst, dst_ref=dst, send_sem=self.send_sem.at[0],
            recv_sem=self.recv_sem.at[slot], device_id=device, device_id_type=MESH,
        ).wait_recv()

    def left(self, src, group, device):
        pltpu.make_async_remote_copy(
            src_ref=src, dst_ref=src, send_sem=self.send_sem.at[group],
            recv_sem=self.recv_sem.at[0], device_id=device, device_id_type=MESH,
        ).wait_send()


def kernel(tok, cot, up, down, out_mixed, out_grad,
           x_all, c_all, wu, wd, stage, terms, sendbuf, landed, hidden, slope, gpre,
           local_sem, send_sem, recv_sem):
    dp = lax.axis_index("dp")
    z = lax.axis_index("mp")
    core = lax.rem(dp, 2)
    chip = lax.div(dp, 2)
    px, py = lax.rem(chip, SIDE), lax.div(chip, SIDE)
    a = px * (1 - core) + py * core
    b = py * (1 - core) + px * core

    def chip_at(a_pos, b_pos):
        return a_pos * (1 + 3 * core) + b_pos * (4 - 3 * core)

    def ring(pos, step):
        return lax.rem(pos + step + SIDE, SIDE)

    def plane(a_pos, b_pos):
        return (chip_at(a_pos, b_pos) * 2 + core, z)

    b0 = lax.rem(z, 2)
    b1 = lax.rem(lax.div(z, 2), 2)
    b2 = lax.rem(lax.div(z, 4), 2)
    b3 = lax.rem(lax.div(z, 8), 2)
    d1, d2, d4, d8 = xor_step(b0, 1), xor_step(b1, 2), xor_step(b2, 4), xor_step(b3, 8)

    def along(step):
        return (dp, z + step)

    sibling = (dp + 1 - 2 * core, z)
    sends = Sends(send_sem, recv_sem)

    mine = pl.ds(pl.multiple_of(core * BLK, BLK), BLK)
    theirs = pl.ds(pl.multiple_of((1 - core) * BLK, BLK), BLK)
    own_rows = pl.ds(pl.multiple_of(core * TOK, TOK), TOK)
    sib_rows = pl.ds(pl.multiple_of((1 - core) * TOK, TOK), TOK)
    own_units = pl.ds(pl.multiple_of(core * HB, HB), HB)
    sib_units = pl.ds(pl.multiple_of((1 - core) * HB, HB), HB)
    acts, alls = (tok, cot), (x_all, c_all)
    weights, gathered = (up, down), (wu, wd)

    barrier = pltpu.get_barrier_semaphore()
    a_up, a_down, b_up, b_down = (
        plane(ring(a, 1), b), plane(ring(a, -1), b), plane(a, ring(b, 1)), plane(a, ring(b, -1)))
    greet = [along(s) for s in (d4 + d8, d4, d2, d1)]
    greet += [a_up, a_down, b_up, b_down, sibling]
    for device in greet:
        pl.semaphore_signal(barrier, inc=1, device_id=device, device_id_type=MESH)
    local = []
    for n in range(2):
        local.append(pltpu.make_async_copy(acts[n].at[:, mine], alls[n].at[0, own_rows, :], local_sem.at[n]))
        local.append(pltpu.make_async_copy(weights[n].at[:, :, own_units], stage.at[n, 0], local_sem.at[2 + n]))
    for copy in local:
        copy.start()

    pl.semaphore_wait(barrier, len(greet))

    swap_act = [sends.slot() for _ in range(2)]
    swap_w = [sends.slot() for _ in range(2)]
    swap_act_group = [sends.group() for _ in range(2)]
    swap_w_group = [sends.group() for _ in range(2)]
    for n in range(2):
        sends.start(acts[n].at[:, theirs], alls[n].at[0, own_rows, :], swap_act_group[n], swap_act[n], sibling)
        sends.start(weights[n].at[:, :, sib_units], stage.at[n, 1], swap_w_group[n], swap_w[n], sibling)

    near_slot = [[sends.slot() for _ in range(2)] for _ in range(2)]
    four_slot = [[sends.slot() for _ in range(2)] for _ in range(2)]
    act_group = [sends.group() for _ in range(2)]
    act_rows = (own_rows, sib_rows)
    act_place = (0, 1, 2, 4, 3)

    def act_send(n, ch, src, dst, slot, device):
        rows = act_rows[ch]
        sends.start(alls[n].at[src, rows, :], alls[n].at[dst, rows, :], act_group[n], slot[n][ch], device)

    def act_four(n, ch):
        sends.arrive(alls[n].at[4, act_rows[ch], :], four_slot[n][ch], sibling)
        act_send(n, ch, 4, 3, near_slot, along(d4 + d8))

    def near_own(n, ch):
        if ch == 0:
            local[2 * n].wait()
        else:
            sends.arrive(alls[n].at[0, sib_rows, :], swap_act[n], sibling)
        act_send(n, ch, 0, 4, four_slot, along(d4))
        act_send(n, ch, 0, 2, near_slot, along(d2))
        act_send(n, ch, 0, 1, near_slot, along(d1))

    def near_end(n, ch):
        sends.arrive(alls[n].at[1:4, act_rows[ch], :], near_slot[n][ch], sibling)

    parts = ((0, 0, 5), (1, 3, 5), (1, 0, 3))
    w_slot = [[sends.slot() for _ in range(12)] for _ in parts]
    w_group = [sends.group() for _ in parts]
    ks = (a, ring(a, -1), ring(a, 1), ring(a, 2))
    lo, hi, whole = pl.ds(0, HB // 2), pl.ds(HB // 2, HB // 2), pl.ds(0, HB)

    def piece(n, a_pos, b_pos, cols):
        rows = pl.ds(pl.multiple_of(chip_at(a_pos, b_pos) * 16, 16), 16)
        array, first, end = parts[n]
        return gathered[array].at[first:end, rows, cols]

    def w_send(n, a_pos, b_pos, cols, slot, device):
        ref = piece(n, a_pos, b_pos, cols)
        sends.start(ref, ref, w_group[n], w_slot[n][slot], device)

    def w_wait(n, a_pos, b_pos, slot):
        sends.arrive(piece(n, a_pos, b_pos, whole), w_slot[n][slot], sibling)

    def w_across(n, k):
        w_send(n, ks[k], b, whole, 3 + k, b_up)
        w_send(n, ks[k], b, whole, 7 + k, b_down)

    def w_join(array):
        local[2 * array + 1].wait()
        sends.arrive(stage.at[array, 1], swap_w[array], sibling)
        first = stage[array, 0].astype(jnp.float32)
        second = stage[array, 1].astype(jnp.float32)
        rows = pl.ds(pl.multiple_of(chip * 16, 16), 16)

        @pl.when(core == 0)
        def _():
            gathered[array][:, rows, :] = jnp.concatenate([first, second], axis=1).astype(jnp.bfloat16)

        @pl.when(core == 1)
        def _():
            gathered[array][:, rows, :] = jnp.concatenate([second, first], axis=1).astype(jnp.bfloat16)

    def w_start(n):
        w_send(n, a, b, whole, 0, a_up)
        w_send(n, a, b, whole, 1, a_down)
        w_across(n, 0)

    def w_near(n):
        w_wait(n, ks[1], b, 0)
        w_send(n, ks[1], b, lo, 2, a_up)
        w_wait(n, ks[2], b, 1)
        w_send(n, ks[2], b, hi, 2, a_down)
        w_across(n, 1)
        w_across(n, 2)

    def w_far(n):
        w_wait(n, ks[3], b, 2)
        w_across(n, 3)

    def w_pass(n, k):
        w_wait(n, ks[k], ring(b, -1), 3 + k)
        w_send(n, ks[k], ring(b, -1), lo, 11, b_up)
        w_wait(n, ks[k], ring(b, 1), 7 + k)
        w_send(n, ks[k], ring(b, 1), hi, 11, b_down)

    def w_end(n):
        array, first, end = parts[n]
        sends.arrive(gathered[array].at[first:end, 0:64, :], w_slot[n][11], sibling)

    TILE = 256

    def product(all_ref, w_ref, cols):
        total = None
        for s in range(TERMS):
            part = jnp.dot(all_ref[act_place[s]], w_ref[s, :, cols], preferred_element_type=jnp.float32)
            total = part if total is None else total + part
        return total

    def forward():
        def body(tile, carry):
            cols = pl.ds(pl.multiple_of(tile * TILE, TILE), TILE)
            pre = product(x_all, wu, cols)
            th = jnp.tanh(ROOT * (pre + CUBE * pre * pre * pre))
            hidden[:, cols] = (0.5 * pre * (1.0 + th)).astype(jnp.bfloat16)
            inner = ROOT * (1.0 + 3.0 * CUBE * pre * pre)
            slope[:, cols] = 0.5 * (1.0 + th) + 0.5 * pre * (1.0 - th * th) * inner
            return carry
        lax.fori_loop(0, HB // TILE, body, 0)

    def backward():
        def body(tile, carry):
            cols = pl.ds(pl.multiple_of(tile * TILE, TILE), TILE)
            gpre[:, cols] = (product(c_all, wd, cols) * slope[:, cols]).astype(jnp.bfloat16)
            return carry
        lax.fori_loop(0, HB // TILE, body, 0)

    def term(o, s):
        act_ref, w_ref = ((hidden, wd), (gpre, wu))[o]
        total = lax.dot_general(
            act_ref[...], w_ref[s], (((1,), (1,)), ((), ())), preferred_element_type=jnp.float32)
        if s in (0, 3):
            terms[o, s // 3] = total
        else:
            sendbuf[o, s] = total.astype(jnp.bfloat16)

    first_slot = [[sends.slot() for _ in range(2)] for _ in range(2)]
    last_slot = [[sends.slot() for _ in range(2)] for _ in range(2)]
    sum_group = [sends.group() for _ in range(2)]
    out_slot = [sends.slot() for _ in range(2)]
    out_group = [sends.group() for _ in range(2)]
    sum_rows = (sib_rows, own_rows)
    outs = (out_mixed, out_grad)
    last = []

    def sum_send(o, ch, s, place, slot, device):
        rows = sum_rows[ch]
        sends.start(sendbuf.at[o, s, rows, :], landed.at[o, place, rows, :], sum_group[o], slot[o][ch], device)

    def sum_eight(o, ch):
        sum_send(o, ch, 4, 3, first_slot, along(d4 + d8))

    def near_two(o, ch):
        sum_send(o, ch, 2, 1, last_slot, along(d2))

    def near_one(o, ch):
        sum_send(o, ch, 1, 0, last_slot, along(d1))

    def near_four(o, ch):
        rows = sum_rows[ch]
        sends.arrive(landed.at[o, 3, rows, :], first_slot[o][ch], sibling)
        total = terms[o, 1, rows, :] + landed[o, 3, rows, :].astype(jnp.float32)
        sendbuf[o, 3, rows, :] = total.astype(jnp.bfloat16)
        sum_send(o, ch, 3, 2, last_slot, along(d4))

    def near_sum(o, ch):
        rows = sum_rows[ch]
        sends.arrive(landed.at[o, 0:3, rows, :], last_slot[o][ch], sibling)
        total = terms[o, 0, rows, :]
        for place in range(3):
            total = total + landed[o, place, rows, :].astype(jnp.float32)
        sendbuf[o, 0, rows, :] = total.astype(jnp.bfloat16)
        if ch == 0:
            sends.start(sendbuf.at[o, 0, sib_rows, :], outs[o].at[:, mine], out_group[o], out_slot[o], sibling)
        else:
            copy = pltpu.make_async_copy(sendbuf.at[o, 0, own_rows, :], outs[o].at[:, mine], local_sem.at[4 + o])
            copy.start()
            last.append(copy)

    T, C, M, G = 0, 1, 0, 1
    UP, DA, DB = 0, 1, 2
    near_own(T,0)
    w_join(0)
    w_start(0)
    near_own(T,1)
    w_join(1)
    w_start(1)
    w_near(0)
    w_pass(0, 0)
    act_four(T,0)
    w_far(0)
    w_start(2)
    act_four(T,1)
    near_own(C,0)
    near_own(C,1)
    w_near(1)
    w_pass(0, 1)
    w_pass(0, 2)
    w_pass(1, 0)
    w_pass(0, 3)
    w_far(1)
    w_near(2)
    w_pass(1, 1)
    w_pass(1, 2)
    w_end(0)
    w_pass(2, 0)
    w_far(2)
    w_pass(1, 3)
    act_four(C,0)
    w_end(1)
    near_end(T,0)
    near_end(T,1)
    forward()
    term(M,4)
    sum_eight(M,0)
    sum_eight(M,1)
    w_pass(2, 1)
    w_pass(2, 2)
    w_pass(2, 3)
    w_end(2)
    act_four(C,1)
    term(M,2)
    near_two(M,0)
    term(M,3)
    near_four(M,0)
    term(M,1)
    near_two(M,1)
    near_one(M,0)
    near_four(M,1)
    near_one(M,1)
    term(M,0)
    near_end(C,0)
    near_end(C,1)
    backward()
    term(G,4)
    sum_eight(G,0)
    sum_eight(G,1)
    term(G,2)
    near_two(G,0)
    term(G,3)
    near_four(G,0)
    near_two(G,1)
    near_four(G,1)
    term(G,1)
    near_one(G,0)
    near_one(G,1)
    term(G,0)
    near_sum(M,0)
    near_sum(M,1)
    near_sum(G,0)
    near_sum(G,1)
    for o in range(2):
        sends.arrive(outs[o].at[:, theirs], out_slot[o], sibling)
    for copy in last:
        copy.wait()
    for n in range(2):
        sends.left(alls[n].at[0, own_rows, :], swap_act_group[n], sibling)
        sends.left(stage.at[n, 1], swap_w_group[n], sibling)
        sends.left(alls[n].at[0:4], act_group[n], sibling)
        sends.left(sendbuf.at[n, 0:4], sum_group[n], sibling)
        sends.left(sendbuf.at[n, 0, sib_rows, :], out_group[n], sibling)
    for n, (array, first, end) in enumerate(parts):
        sends.left(gathered[array].at[first:end, 0:240, :], w_group[n], sibling)
    assert sends.groups == SEND_SEMS and sends.received == RECV_SEMS


def on_device(tokens, cotangent, up_weight, down_weight):
    any_spec = pl.BlockSpec(memory_space=pl.ANY)
    hbm_spec = pl.BlockSpec(memory_space=pltpu.HBM)
    bf, f32 = jnp.bfloat16, jnp.float32
    return pl.pallas_call(
        kernel,
        out_shape=[jax.ShapeDtypeStruct(tokens.shape, bf)] * 2,
        in_specs=[hbm_spec] * 4,
        out_specs=[any_spec] * 2,
        scratch_shapes=[
            pltpu.VMEM((TERMS, 2 * TOK, BLK), bf),
            pltpu.VMEM((TERMS, 2 * TOK, BLK), bf),
            pltpu.VMEM((TERMS, BLK, HB), bf),
            pltpu.VMEM((TERMS, BLK, HB), bf),
            pltpu.VMEM((2, 2, TERMS, 8, HB), bf),
            pltpu.VMEM((2, 2, 2 * TOK, BLK), f32),
            pltpu.VMEM((2, TERMS, 2 * TOK, BLK), bf),
            pltpu.VMEM((2, 4, 2 * TOK, BLK), bf),
            pltpu.VMEM((2 * TOK, HB), bf),
            pltpu.VMEM((2 * TOK, HB), f32),
            pltpu.VMEM((2 * TOK, HB), bf),
            pltpu.SemaphoreType.DMA((6,)),
            pltpu.SemaphoreType.DMA((SEND_SEMS,)),
            pltpu.SemaphoreType.DMA((RECV_SEMS,)),
        ],
        compiler_params=pltpu.CompilerParams(
            collective_id=0, has_side_effects=True, vmem_limit_bytes=48 * 1024 * 1024),
    )(*[pltpu.with_memory_space_constraint(v, pltpu.HBM) for v in (tokens, cotangent, up_weight, down_weight)])


def solution(mesh):
    act, weight = P("dp", "mp"), P(None, "dp", "mp")
    return jax.shard_map(
        on_device, mesh=mesh, in_specs=(act, act, weight, weight), out_specs=(act, act), check_vma=False)
```

time: 100 us -> 93 us (0.930)
  the two profiles are of different devices: /device:TPU:32 before, /device:TPU:65 now
where the time goes in v3:
time: 93 us; the launch traced here: 92.9 us
  Pallas kernels  90.9 us (98%)
  local copies, waits for them, and re-layouts  1.31 us (1%)
    pallas_call x1, Pallas kernels, on_device(): pl.pallas_call(kernel, out_shape=[jax.ShapeDtypeStruct(tokens.shape, bf)]...  90.9 us

profile of v3, /device:TPU:65, one launch (start us, length us, event | category | flops | bytes accessed | tf_op | source)
XLA Modules:
  0.0 92.9 jit_solution(9812492924022648043)
XLA Ops:
  0.6 90.9 %shard_map.59 = (bf16[128,512]{1,0:T(8,128)(2,1)S(1)}, bf16[128,512]{1,0:T(8,128)(2,1)S(1)}) custom-call(bf16[128,512]{1,0:T(8,128)(2,1)} %tok.1, bf16[128,512]{1,0:T(8,128)(2,1)} %cot.1, bf16[5,8,2048]{2,1,0:T(8,128)(2,1)} %up.1, bf16[5,8,2048]{2,1,0:T(8,128)(2,1)} %down.1), custom_call_target="tpu_custom_call" | custom-call | tf_op jit(solution)/shard_map/pallas_call | solution.py:382
  91.6 0.7 copy.8
  92.2 0.7 copy.9

commit v4 on v3

--- a/solution.py
+++ b/solution.py
@@ -15,7 +15,7 @@
 MESH = pl.DeviceIdType.MESH
 ROOT = math.sqrt(2.0 / math.pi)
 CUBE = 0.044715
-SEND_SEMS, RECV_SEMS = 13, 58
+SEND_SEMS, RECV_SEMS = 13, 66
 
 
 def xor_step(bit, amount):
@@ -54,7 +54,7 @@
         ).wait_send()
 
 
-def kernel(tok, cot, up, down, out_mixed, out_grad,
+def kernel(tok, cot, up, down, both,
            x_all, c_all, wu, wd, stage, terms, sendbuf, landed, hidden, slope, gpre,
            local_sem, send_sem, recv_sem):
     dp = lax.axis_index("dp")
@@ -90,6 +90,12 @@
     theirs = pl.ds(pl.multiple_of((1 - core) * BLK, BLK), BLK)
     own_rows = pl.ds(pl.multiple_of(core * TOK, TOK), TOK)
     sib_rows = pl.ds(pl.multiple_of((1 - core) * TOK, TOK), TOK)
+    cuts = (1, 1, 2, 2)
+
+    def pieces(base, count):
+        step = TOK // count
+        return [pl.ds(pl.multiple_of(base * TOK + i * step, step), step) for i in range(count)]
+
     own_units = pl.ds(pl.multiple_of(core * HB, HB), HB)
     sib_units = pl.ds(pl.multiple_of((1 - core) * HB, HB), HB)
     acts, alls = (tok, cot), (x_all, c_all)
@@ -119,31 +125,31 @@
         sends.start(acts[n].at[:, theirs], alls[n].at[0, own_rows, :], swap_act_group[n], swap_act[n], sibling)
         sends.start(weights[n].at[:, :, sib_units], stage.at[n, 1], swap_w_group[n], swap_w[n], sibling)
 
-    near_slot = [[sends.slot() for _ in range(2)] for _ in range(2)]
-    four_slot = [[sends.slot() for _ in range(2)] for _ in range(2)]
+    act_rows = [pieces(core, cuts[n]) + pieces(1 - core, cuts[n]) for n in range(2)]
+    near_slot = [[sends.slot() for _ in rows] for rows in act_rows]
+    four_slot = [[sends.slot() for _ in rows] for rows in act_rows]
     act_group = [sends.group() for _ in range(2)]
-    act_rows = (own_rows, sib_rows)
     act_place = (0, 1, 2, 4, 3)
 
     def act_send(n, ch, src, dst, slot, device):
-        rows = act_rows[ch]
+        rows = act_rows[n][ch]
         sends.start(alls[n].at[src, rows, :], alls[n].at[dst, rows, :], act_group[n], slot[n][ch], device)
 
     def act_four(n, ch):
-        sends.arrive(alls[n].at[4, act_rows[ch], :], four_slot[n][ch], sibling)
+        sends.arrive(alls[n].at[4, act_rows[n][ch], :], four_slot[n][ch], sibling)
         act_send(n, ch, 4, 3, near_slot, along(d4 + d8))
 
     def near_own(n, ch):
         if ch == 0:
             local[2 * n].wait()
-        else:
+        elif ch == cuts[n]:
             sends.arrive(alls[n].at[0, sib_rows, :], swap_act[n], sibling)
         act_send(n, ch, 0, 4, four_slot, along(d4))
         act_send(n, ch, 0, 2, near_slot, along(d2))
         act_send(n, ch, 0, 1, near_slot, along(d1))
 
     def near_end(n, ch):
-        sends.arrive(alls[n].at[1:4, act_rows[ch], :], near_slot[n][ch], sibling)
+        sends.arrive(alls[n].at[1:4, act_rows[n][ch], :], near_slot[n][ch], sibling)
 
     parts = ((0, 0, 5), (1, 3, 5), (1, 0, 3))
     w_slot = [[sends.slot() for _ in range(12)] for _ in parts]
@@ -245,17 +251,17 @@
         else:
             sendbuf[o, s] = total.astype(jnp.bfloat16)
 
-    first_slot = [[sends.slot() for _ in range(2)] for _ in range(2)]
-    last_slot = [[sends.slot() for _ in range(2)] for _ in range(2)]
+    sum_rows = [pieces(1 - core, cuts[2 + o]) + pieces(core, cuts[2 + o]) for o in range(2)]
+    first_slot = [[sends.slot() for _ in rows] for rows in sum_rows]
+    last_slot = [[sends.slot() for _ in rows] for rows in sum_rows]
     sum_group = [sends.group() for _ in range(2)]
     out_slot = [sends.slot() for _ in range(2)]
     out_group = [sends.group() for _ in range(2)]
-    sum_rows = (sib_rows, own_rows)
-    outs = (out_mixed, out_grad)
+    outs = (both.at[0], both.at[1])
     last = []
 
     def sum_send(o, ch, s, place, slot, device):
-        rows = sum_rows[ch]
+        rows = sum_rows[o][ch]
         sends.start(sendbuf.at[o, s, rows, :], landed.at[o, place, rows, :], sum_group[o], slot[o][ch], device)
 
     def sum_eight(o, ch):
@@ -268,42 +274,44 @@
         sum_send(o, ch, 1, 0, last_slot, along(d1))
 
     def near_four(o, ch):
-        rows = sum_rows[ch]
+        rows = sum_rows[o][ch]
         sends.arrive(landed.at[o, 3, rows, :], first_slot[o][ch], sibling)
         total = terms[o, 1, rows, :] + landed[o, 3, rows, :].astype(jnp.float32)
         sendbuf[o, 3, rows, :] = total.astype(jnp.bfloat16)
         sum_send(o, ch, 3, 2, last_slot, along(d4))
 
     def near_sum(o, ch):
-        rows = sum_rows[ch]
+        rows = sum_rows[o][ch]
         sends.arrive(landed.at[o, 0:3, rows, :], last_slot[o][ch], sibling)
         total = terms[o, 0, rows, :]
         for place in range(3):
             total = total + landed[o, place, rows, :].astype(jnp.float32)
         sendbuf[o, 0, rows, :] = total.astype(jnp.bfloat16)
-        if ch == 0:
-            sends.start(sendbuf.at[o, 0, sib_rows, :], outs[o].at[:, mine], out_group[o], out_slot[o], sibling)
+        here = pl.ds(ch % cuts[2 + o] * (TOK // cuts[2 + o]), TOK // cuts[2 + o])
+        place = outs[o].at[here, mine]
+        if ch < cuts[2 + o]:
+            sends.start(sendbuf.at[o, 0, rows, :], place, out_group[o], out_slot[o], sibling)
         else:
-            copy = pltpu.make_async_copy(sendbuf.at[o, 0, own_rows, :], outs[o].at[:, mine], local_sem.at[4 + o])
+            copy = pltpu.make_async_copy(sendbuf.at[o, 0, rows, :], place, local_sem.at[4 + 2 * o + ch % cuts[2 + o]])
             copy.start()
             last.append(copy)
 
     T, C, M, G = 0, 1, 0, 1
     UP, DA, DB = 0, 1, 2
-    near_own(T,0)
+    near_own(T, 0)
     w_join(0)
     w_start(0)
-    near_own(T,1)
+    near_own(T, 1)
     w_join(1)
     w_start(1)
     w_near(0)
     w_pass(0, 0)
-    act_four(T,0)
+    act_four(T, 0)
     w_far(0)
     w_start(2)
-    act_four(T,1)
-    near_own(C,0)
-    near_own(C,1)
+    act_four(T, 1)
+    near_own(C, 0)
+    near_own(C, 1)
     w_near(1)
     w_pass(0, 1)
     w_pass(0, 2)
@@ -317,49 +325,69 @@
     w_pass(2, 0)
     w_far(2)
     w_pass(1, 3)
-    act_four(C,0)
+    act_four(C, 0)
     w_end(1)
-    near_end(T,0)
-    near_end(T,1)
+    near_end(T, 0)
+    near_end(T, 1)
     forward()
     term(M,4)
-    sum_eight(M,0)
-    sum_eight(M,1)
+    sum_eight(M, 0)
+    sum_eight(M, 1)
+    sum_eight(M, 2)
+    sum_eight(M, 3)
     w_pass(2, 1)
     w_pass(2, 2)
     w_pass(2, 3)
     w_end(2)
-    act_four(C,1)
+    act_four(C, 1)
     term(M,2)
-    near_two(M,0)
+    near_two(M, 0)
+    near_two(M, 1)
     term(M,3)
-    near_four(M,0)
+    near_four(M, 0)
+    near_four(M, 1)
     term(M,1)
-    near_two(M,1)
-    near_one(M,0)
-    near_four(M,1)
-    near_one(M,1)
+    near_two(M, 2)
+    near_two(M, 3)
+    near_one(M, 0)
+    near_one(M, 1)
+    near_four(M, 2)
+    near_four(M, 3)
+    near_one(M, 2)
+    near_one(M, 3)
     term(M,0)
-    near_end(C,0)
-    near_end(C,1)
+    near_end(C, 0)
+    near_end(C, 1)
     backward()
     term(G,4)
-    sum_eight(G,0)
-    sum_eight(G,1)
+    sum_eight(G, 0)
+    sum_eight(G, 1)
+    sum_eight(G, 2)
+    sum_eight(G, 3)
     term(G,2)
-    near_two(G,0)
+    near_two(G, 0)
+    near_two(G, 1)
     term(G,3)
-    near_four(G,0)
-    near_two(G,1)
-    near_four(G,1)
+    near_four(G, 0)
+    near_four(G, 1)
+    near_two(G, 2)
+    near_two(G, 3)
+    near_four(G, 2)
+    near_four(G, 3)
     term(G,1)
-    near_one(G,0)
-    near_one(G,1)
+    near_one(G, 0)
+    near_one(G, 1)
+    near_one(G, 2)
+    near_one(G, 3)
     term(G,0)
-    near_sum(M,0)
-    near_sum(M,1)
-    near_sum(G,0)
-    near_sum(G,1)
+    near_sum(M, 0)
+    near_sum(M, 1)
+    near_sum(M, 2)
+    near_sum(M, 3)
+    near_sum(G, 0)
+    near_sum(G, 1)
+    near_sum(G, 2)
+    near_sum(G, 3)
     for o in range(2):
         sends.arrive(outs[o].at[:, theirs], out_slot[o], sibling)
     for copy in last:
@@ -372,18 +400,17 @@
         sends.left(sendbuf.at[n, 0, sib_rows, :], out_group[n], sibling)
     for n, (array, first, end) in enumerate(parts):
         sends.left(gathered[array].at[first:end, 0:240, :], w_group[n], sibling)
-    assert sends.groups == SEND_SEMS and sends.received == RECV_SEMS
 
 
 def on_device(tokens, cotangent, up_weight, down_weight):
     any_spec = pl.BlockSpec(memory_space=pl.ANY)
     hbm_spec = pl.BlockSpec(memory_space=pltpu.HBM)
     bf, f32 = jnp.bfloat16, jnp.float32
-    return pl.pallas_call(
+    both = pl.pallas_call(
         kernel,
-        out_shape=[jax.ShapeDtypeStruct(tokens.shape, bf)] * 2,
+        out_shape=jax.ShapeDtypeStruct((2,) + tokens.shape, bf),
         in_specs=[hbm_spec] * 4,
-        out_specs=[any_spec] * 2,
+        out_specs=any_spec,
         scratch_shapes=[
             pltpu.VMEM((TERMS, 2 * TOK, BLK), bf),
             pltpu.VMEM((TERMS, 2 * TOK, BLK), bf),
@@ -396,13 +423,14 @@
             pltpu.VMEM((2 * TOK, HB), bf),
             pltpu.VMEM((2 * TOK, HB), f32),
             pltpu.VMEM((2 * TOK, HB), bf),
-            pltpu.SemaphoreType.DMA((6,)),
+            pltpu.SemaphoreType.DMA((8,)),
             pltpu.SemaphoreType.DMA((SEND_SEMS,)),
             pltpu.SemaphoreType.DMA((RECV_SEMS,)),
         ],
         compiler_params=pltpu.CompilerParams(
             collective_id=0, has_side_effects=True, vmem_limit_bytes=48 * 1024 * 1024),
     )(*[pltpu.with_memory_space_constraint(v, pltpu.HBM) for v in (tokens, cotangent, up_weight, down_weight)])
+    return both[0], both[1]
 
 
 def solution(mesh):

time: 93 us -> 91.6 us (0.985)
    unnamed x2 -> x0, local copies, waits for them, and re-layouts: 1.31 us -> none
where the time goes in v4:
time: 91.6 us; the launch traced here: 91.5 us
  Pallas kernels  90.2 us (98%)
    pallas_call x1, Pallas kernels, on_device(): pl.pallas_call(kernel, out_shape=jax.ShapeDtypeStruct((2,) + tokens.shape...  90.2 us

profile of v4, /device:TPU:65, one launch (start us, length us, event | category | flops | bytes accessed | tf_op | source)
XLA Modules:
  0.0 91.5 jit_solution(14604327900028571656)
XLA Ops:
  0.6 90.2 %shard_map.59 = bf16[2,128,512]{2,1,0:T(8,128)(2,1)S(1)} custom-call(bf16[128,512]{1,0:T(8,128)(2,1)} %tok.1, bf16[128,512]{1,0:T(8,128)(2,1)} %cot.1, bf16[5,8,2048]{2,1,0:T(8,128)(2,1)} %up.1, bf16[5,8,2048]{2,1,0:T(8,128)(2,1)} %down.1), custom_call_target="tpu_custom_call" | custom-call | tf_op jit(solution)/shard_map/pallas_call | solution.py:409
  90.8 0.7 slice_bitcast_fusion

commit v5 on v4

--- a/solution.py
+++ b/solution.py
@@ -151,7 +151,7 @@
     def near_end(n, ch):
         sends.arrive(alls[n].at[1:4, act_rows[n][ch], :], near_slot[n][ch], sibling)
 
-    parts = ((0, 0, 5), (1, 3, 5), (1, 0, 3))
+    parts = ((0, 0, 5), (1, 2, 5), (1, 0, 2))
     w_slot = [[sends.slot() for _ in range(12)] for _ in parts]
     w_group = [sends.group() for _ in parts]
     ks = (a, ring(a, -1), ring(a, 1), ring(a, 2))
@@ -335,20 +335,20 @@
     sum_eight(M, 1)
     sum_eight(M, 2)
     sum_eight(M, 3)
+    term(M,2)
+    near_two(M, 0)
+    near_two(M, 1)
+    near_two(M, 2)
+    near_two(M, 3)
     w_pass(2, 1)
+    act_four(C, 1)
     w_pass(2, 2)
     w_pass(2, 3)
     w_end(2)
-    act_four(C, 1)
-    term(M,2)
-    near_two(M, 0)
-    near_two(M, 1)
     term(M,3)
     near_four(M, 0)
     near_four(M, 1)
     term(M,1)
-    near_two(M, 2)
-    near_two(M, 3)
     near_one(M, 0)
     near_one(M, 1)
     near_four(M, 2)

time: 91.6 us -> 91.1 us (level)
  the two profiles are of different devices: /device:TPU:65 before, /device:TPU:39 now
where the time goes in v5:
time: 91.1 us; the launch traced here: 91 us
  Pallas kernels  89.7 us (98%)
    pallas_call x1, Pallas kernels, on_device(): pl.pallas_call(kernel, out_shape=jax.ShapeDtypeStruct((2,) + tokens.shape...  89.7 us

profile of v5, /device:TPU:39, one launch (start us, length us, event | category | flops | bytes accessed | tf_op | source)
XLA Modules:
  0.0 91.0 jit_solution(2489302720181194875)
XLA Ops:
  0.6 89.7 %shard_map.59 = bf16[2,128,512]{2,1,0:T(8,128)(2,1)S(1)} custom-call(bf16[128,512]{1,0:T(8,128)(2,1)} %tok.1, bf16[128,512]{1,0:T(8,128)(2,1)} %cot.1, bf16[5,8,2048]{2,1,0:T(8,128)(2,1)} %up.1, bf16[5,8,2048]{2,1,0:T(8,128)(2,1)} %down.1), custom_call_target="tpu_custom_call" | custom-call | tf_op jit(solution)/shard_map/pallas_call | solution.py:409
  90.3 0.7 slice_bitcast_fusion

commit v6 on v5

--- a/solution.py
+++ b/solution.py
@@ -15,7 +15,7 @@
 MESH = pl.DeviceIdType.MESH
 ROOT = math.sqrt(2.0 / math.pi)
 CUBE = 0.044715
-SEND_SEMS, RECV_SEMS = 13, 66
+SEND_SEMS, RECV_SEMS = 13, 54
 
 
 def xor_step(bit, amount):
@@ -152,7 +152,7 @@
         sends.arrive(alls[n].at[1:4, act_rows[n][ch], :], near_slot[n][ch], sibling)
 
     parts = ((0, 0, 5), (1, 2, 5), (1, 0, 2))
-    w_slot = [[sends.slot() for _ in range(12)] for _ in parts]
+    w_slot = [[sends.slot() for _ in range(8)] for _ in parts]
     w_group = [sends.group() for _ in parts]
     ks = (a, ring(a, -1), ring(a, 1), ring(a, 2))
     lo, hi, whole = pl.ds(0, HB // 2), pl.ds(HB // 2, HB // 2), pl.ds(0, HB)
@@ -171,7 +171,7 @@
 
     def w_across(n, k):
         w_send(n, ks[k], b, whole, 3 + k, b_up)
-        w_send(n, ks[k], b, whole, 7 + k, b_down)
+        w_send(n, ks[k], b, whole, 3 + k, b_down)
 
     def w_join(array):
         local[2 * array + 1].wait()
@@ -206,14 +206,14 @@
         w_across(n, 3)
 
     def w_pass(n, k):
-        w_wait(n, ks[k], ring(b, -1), 3 + k)
-        w_send(n, ks[k], ring(b, -1), lo, 11, b_up)
-        w_wait(n, ks[k], ring(b, 1), 7 + k)
-        w_send(n, ks[k], ring(b, 1), hi, 11, b_down)
+        array, first, end = parts[n]
+        sends.arrive(gathered[array].at[first:end, 0:32, :], w_slot[n][3 + k], sibling)
+        w_send(n, ks[k], ring(b, -1), lo, 7, b_up)
+        w_send(n, ks[k], ring(b, 1), hi, 7, b_down)
 
     def w_end(n):
         array, first, end = parts[n]
-        sends.arrive(gathered[array].at[first:end, 0:64, :], w_slot[n][11], sibling)
+        sends.arrive(gathered[array].at[first:end, 0:64, :], w_slot[n][7], sibling)
 
     TILE = 256
 

time: 91.1 us -> 91 us (level)
  no operation moved by 1% of the time
where the time goes in v6:
time: 91 us; the launch traced here: 90.9 us
  Pallas kernels  89.5 us (98%)
    pallas_call x1, Pallas kernels, on_device(): pl.pallas_call(kernel, out_shape=jax.ShapeDtypeStruct((2,) + tokens.shape...  89.5 us

profile of v6, /device:TPU:39, one launch (start us, length us, event | category | flops | bytes accessed | tf_op | source)
XLA Modules:
  0.0 90.9 jit_solution(14116688398266169907)
XLA Ops:
  0.6 89.5 %shard_map.59 = bf16[2,128,512]{2,1,0:T(8,128)(2,1)S(1)} custom-call(bf16[128,512]{1,0:T(8,128)(2,1)} %tok.1, bf16[128,512]{1,0:T(8,128)(2,1)} %cot.1, bf16[5,8,2048]{2,1,0:T(8,128)(2,1)} %up.1, bf16[5,8,2048]{2,1,0:T(8,128)(2,1)} %down.1), custom_call_target="tpu_custom_call" | custom-call | tf_op jit(solution)/shard_map/pallas_call | solution.py:409
  90.2 0.7 slice_bitcast_fusion

commit v7 on v6

--- a/solution.py
+++ b/solution.py
@@ -15,7 +15,7 @@
 MESH = pl.DeviceIdType.MESH
 ROOT = math.sqrt(2.0 / math.pi)
 CUBE = 0.044715
-SEND_SEMS, RECV_SEMS = 13, 54
+SEND_SEMS, RECV_SEMS = 13, 51
 
 
 def xor_step(bit, amount):
@@ -152,7 +152,7 @@
         sends.arrive(alls[n].at[1:4, act_rows[n][ch], :], near_slot[n][ch], sibling)
 
     parts = ((0, 0, 5), (1, 2, 5), (1, 0, 2))
-    w_slot = [[sends.slot() for _ in range(8)] for _ in parts]
+    w_slot = [[sends.slot() for _ in range(7)] for _ in parts]
     w_group = [sends.group() for _ in parts]
     ks = (a, ring(a, -1), ring(a, 1), ring(a, 2))
     lo, hi, whole = pl.ds(0, HB // 2), pl.ds(HB // 2, HB // 2), pl.ds(0, HB)
@@ -190,13 +190,13 @@
 
     def w_start(n):
         w_send(n, a, b, whole, 0, a_up)
-        w_send(n, a, b, whole, 1, a_down)
+        w_send(n, a, b, whole, 0, a_down)
         w_across(n, 0)
 
     def w_near(n):
-        w_wait(n, ks[1], b, 0)
+        array, first, end = parts[n]
+        sends.arrive(gathered[array].at[first:end, 0:32, :], w_slot[n][0], sibling)
         w_send(n, ks[1], b, lo, 2, a_up)
-        w_wait(n, ks[2], b, 1)
         w_send(n, ks[2], b, hi, 2, a_down)
         w_across(n, 1)
         w_across(n, 2)
@@ -208,12 +208,12 @@
     def w_pass(n, k):
         array, first, end = parts[n]
         sends.arrive(gathered[array].at[first:end, 0:32, :], w_slot[n][3 + k], sibling)
-        w_send(n, ks[k], ring(b, -1), lo, 7, b_up)
-        w_send(n, ks[k], ring(b, 1), hi, 7, b_down)
+        w_send(n, ks[k], ring(b, -1), lo, 1, b_up)
+        w_send(n, ks[k], ring(b, 1), hi, 1, b_down)
 
     def w_end(n):
         array, first, end = parts[n]
-        sends.arrive(gathered[array].at[first:end, 0:64, :], w_slot[n][7], sibling)
+        sends.arrive(gathered[array].at[first:end, 0:64, :], w_slot[n][1], sibling)
 
     TILE = 256
 

time: 91 us -> 90.8 us (level)
  the two profiles are of different devices: /device:TPU:39 before, /device:TPU:38 now
where the time goes in v7:
time: 90.8 us; the launch traced here: 90.7 us
  Pallas kernels  89.4 us (98%)
    pallas_call x1, Pallas kernels, on_device(): pl.pallas_call(kernel, out_shape=jax.ShapeDtypeStruct((2,) + tokens.shape...  89.4 us

profile of v7, /device:TPU:38, one launch (start us, length us, event | category | flops | bytes accessed | tf_op | source)
XLA Modules:
  0.0 90.7 jit_solution(13311443958123603752)
XLA Ops:
  0.6 89.4 %shard_map.59 = bf16[2,128,512]{2,1,0:T(8,128)(2,1)S(1)} custom-call(bf16[128,512]{1,0:T(8,128)(2,1)} %tok.1, bf16[128,512]{1,0:T(8,128)(2,1)} %cot.1, bf16[5,8,2048]{2,1,0:T(8,128)(2,1)} %up.1, bf16[5,8,2048]{2,1,0:T(8,128)(2,1)} %down.1), custom_call_target="tpu_custom_call" | custom-call | tf_op jit(solution)/shard_map/pallas_call | solution.py:409
  90.0 0.7 slice_bitcast_fusion
